TPU v7x, 128 devices: a whole 4x4x4 slice. The times are simulated.
128 devices in a mesh: row: 8 (over z, y_hi), col: 16 (over y_lo, x, core).
Axes of the slice: x: 4, y: 4 (y_hi: 2, y_lo: 2; y = y_hi * 2 + y_lo), z: 4, core: 2. Of those that a mesh axis runs over, the one named last changes fastest.
Arguments:
- col_data: bfloat16 [512, 4, 128, 128], P(('row', 'col')), may hold values from -0.029907227 to 0.029907227
- col_scale: bfloat16 [512, 128], P(('row', 'col')), may hold values from 0.0099487305 to 100
- row_ids: int32 [512, 4], P(('row', 'col')), may hold values from 0 to 31, as said below
- live_rows: int32 [512], P(('row', 'col')), may hold values from 1 to 4
- live_blocks: int32 [128], P(('row', 'col')), may hold values from 1 to 4, as said below
- row_reg: float32 [4096], replicated, may hold values from 0.05 to 0.5
Outputs:
- factored: float32 [4096, 4096], P('row', 'col')
Inputs may be any that keep to these rules, and one draw needn't show every extreme that they name: row_ids[c, k] % 4 == k, and (row_ids[c, k] // 4) % 4 == (c % 4) % 4 for every column block c and slot k. `live_blocks`: one device has exactly 4 column blocks.
All inputs are finite; a program needn't handle non-finite values.
Results may differ from a plain program's by a relative error of at most 0.0003.
Values may be sent and summed in bfloat16 or wider, within the bound.
A program may use at most 128 MiB of HBM per device.

v0:
```python
import jax
import jax.numpy as jnp
from jax import lax
from jax.sharding import PartitionSpec as P

ORDER = 4096
PW = 512


def body(col_data, col_scale, row_ids, live_rows, live_blocks, row_reg):
    nrow = lax.axis_size("row")
    ncol = lax.axis_size("col")
    prow = lax.axis_index("row")
    pcol = lax.axis_index("col")
    slots, depth, height, width = col_data.shape
    nblock = ORDER // height
    nbl_here = nblock // nrow
    nbc_here = nblock // ncol
    panel_blocks = PW // height
    slot_on = jnp.arange(slots) < live_blocks[0]
    piece_on = jnp.arange(depth)[None, :] < live_rows[:, None]
    keep = (slot_on[:, None] & piece_on).astype(jnp.bfloat16)
    cleaned = col_data * keep[:, :, None, None]
    ids_wire = row_ids.astype(jnp.bfloat16)
    empty = jnp.zeros((nbl_here, nblock, height, height), jnp.float32)
    data = lax.all_gather(cleaned, "row", axis=0, tiled=True)
    scale = lax.all_gather(col_scale, "row", axis=0, tiled=True)
    ids = lax.all_gather(ids_wire, "row", axis=0, tiled=True)
    ids = ids.astype(jnp.int32)
    pick = prow % depth
    left = lax.dynamic_index_in_dim(data, pick, 1, keepdims=False)
    left_id = lax.dynamic_index_in_dim(ids, pick, 1, keepdims=False)
    owned = (left_id % nrow == prow).astype(jnp.float32)
    scaled = (
        left.astype(jnp.float32) * scale.astype(jnp.float32)[:, None, :] * owned[:, None, None]
    ).astype(jnp.bfloat16)
    product = jnp.einsum("nbw,nkcw->nkbc", scaled, data, preferred_element_type=jnp.float32)
    row_pos = left_id // nrow
    col_pos = ids % ncol * nbc_here + ids // ncol
    partial_value = empty.at[row_pos[:, None], col_pos].add(product)
    owned_blocks = lax.psum_scatter(partial_value, "col", scatter_dimension=1, tiled=True)
    global_row = jnp.arange(nbl_here) * nrow + prow
    global_col = jnp.arange(nbc_here) * ncol + pcol
    on_diag = (global_row[:, None] == global_col[None, :]).astype(jnp.float32)
    reg_rows = row_reg.reshape(nblock, height)[global_row]
    eye_block = jnp.eye(height, dtype=jnp.float32)
    owned_blocks = owned_blocks + on_diag[:, :, None, None] * (
        reg_rows[:, None, :, None] * eye_block[None, None]
    )
    slab = lax.all_gather(owned_blocks[:, :1], "col", axis=1, tiled=True)
    panel_here = slab[:, :panel_blocks].transpose(0, 2, 1, 3).reshape(nbl_here * height, PW)
    every = lax.all_gather(panel_here, "row", axis=0, tiled=True)
    natural = (
        every.reshape(nrow, nbl_here, height, PW).transpose(1, 0, 2, 3).reshape(nblock * height, PW)
    )
    lower = jnp.linalg.cholesky(natural[:PW])
    factor = jax.scipy.linalg.solve_triangular(lower, natural.T, lower=True).T
    factor_blocks = factor.reshape(nblock, height, PW)
    left_rows = factor_blocks[jnp.arange(nbl_here) * nrow + prow]
    col_rows = factor_blocks[jnp.arange(nbc_here) * ncol + pcol]
    update = jnp.einsum("lbk,cdk->lcbd", left_rows, col_rows, precision=lax.Precision.HIGHEST)
    trailing = owned_blocks - update
    panel_piece = lax.dynamic_slice_in_dim(
        left_rows, jnp.minimum(pcol, panel_blocks - 1) * height, height, 2
    )
    upper_zero = jnp.where(
        global_row[:, None, None, None] < panel_blocks, jnp.zeros_like(trailing), trailing
    )
    result = jnp.where(
        global_col[None, :, None, None] < panel_blocks, panel_piece[:, None], upper_zero
    )
    return result.transpose(0, 2, 1, 3).reshape(nbl_here * height, nbc_here * height)


def solution(mesh):
    return jax.shard_map(
        body,
        mesh=mesh,
        in_specs=(
            P(("row", "col"), None, None, None),
            P(("row", "col"), None),
            P(("row", "col"), None),
            P(("row", "col")),
            P(("row", "col")),
            P(),
        ),
        out_specs=P("row", "col"),
        check_vma=False,
    )
```

profile of v0, /device:TPU:0, one launch (start us, length us, event | category | flops | bytes accessed | tf_op | source)
XLA Modules:
  0.0 572.7 jit_solution(10383694338191077686)
XLA Ops:
  10.7 24.9 %all-gather = bf16[8,4,4]{2,1,0:T(4,128)(2,1)S(1)} all-gather(bf16[1,4,4]{2,1,0:T(4,128)(2,1)S(1)} %convert_bitcast_fusion), channel_id=1, replica_groups=mesh['row'=8,'col'=16] {'row'}, dimensions={0}, use_global_device_ids=true | all-gather | bytes 288 | tf_op jit(solution)/shard_map/all_gather | solution.py:28
  35.8 18.4 %all-gather.1 = bf16[8,4,128]{2,1,0:T(4,128)(2,1)S(1)} all-gather(bf16[1,4,128]{2,1,0:T(4,128)(2,1)} %bitcast.156), channel_id=1, replica_groups=mesh['row'=8,'col'=16] {'row'}, dimensions={0}, use_global_device_ids=true | all-gather | bytes 9216 | tf_op jit(solution)/shard_map/all_gather | solution.py:27
  54.5 29.7 %all-gather.6.cloned.1.call-done = bf16[32,4,128,128]{3,2,1,0:T(8,128)(2,1)} async-done(((bf16[4,4,128,128]{3,2,1,0:T(8,128)(2,1)}), bf16[32,4,128,128]{3,2,1,0:T(8,128)(2,1)}) %all-gather.6.cloned.1.call-update) | async-done | bytes 4194320 | tf_op jit(solution)/shard_map/all_gather | solution.py:26
  84.2 7.0 %fusion.21 = f32[32,4,128,128]{3,2,1,0:T(8,128)} fusion(bf16[32,4,128,128]{3,2,1,0:T(8,128)(2,1)} %all-gather.6.cloned.1.call-done, f32[32]{0:T(128)S(1)} %get-tuple-element.37, f32[32,128]{1,0:T(8,128)S(1)} %convert.2, s32[]{:T(128)S(6)} %select_n.87), kind=kOutput, calls=%fused_computation.37 | convolution fusion | flops 538968064 | bytes 13648004 | tf_op jit(solution)/shard_map/nbw,nkcw->nkbc/dot_general | solution.py:37
  91.2 9.0 %copy.40 = f32[128,128,128]{2,1,0:T(8,128)} copy(f32[128,128,128]{1,2,0:T(8,128)} %bitcast.147) | data formatting | bytes 16777216 | tf_op jit(solution)/shard_map/nbw,nkcw->nkbc/transpose | solution.py:37
  100.2 4.3 broadcast_in_dim.26
  104.5 27.7 %scatter_fusion = f32[4,32,128,128]{3,2,1,0:T(8,128)} fusion(f32[4,32,128,128]{3,2,1,0:T(8,128)} %broadcast_in_dim.26, s32[128]{0:T(128)S(1)} %reshape.283, f32[128,128,128]{2,1,0:T(8,128)} %copy.40), kind=kCustom, calls=%fused_computation.3 | custom fusion | flops 2097152 | bytes 25166848 | tf_op jit(solution)/shard_map/scatter-add | solution.py:40
  132.2 9.0 %copy.41 = f32[4,32,128,128]{2,3,0,1:T(8,128)} copy(f32[4,32,128,128]{3,2,1,0:T(8,128)} %scatter_fusion) | data formatting | bytes 16777216 | tf_op jit(solution)/shard_map/scatter-add | solution.py:40
  142.1 71.5 %reduce-scatter.2.cloned.1.call-done = f32[4,2,128,128]{2,3,0,1:T(8,128)} async-done(((f32[4,32,128,128]{2,3,0,1:T(8,128)}), f32[4,2,128,128]{2,3,0,1:T(8,128)}) %reduce-scatter.2.cloned.1.call-update) | async-done | bytes 524304 | tf_op jit(solution)/shard_map/reduce_scatter | solution.py:41
  215.7 36.0 %all-gather.8.cloned.1.call-done = f32[4,16,128,128]{3,2,0,1:T(8,128)} async-done(((f32[4,1,128,128]{3,2,0,1:T(8,128)}), f32[4,16,128,128]{3,2,0,1:T(8,128)}) %all-gather.8.cloned.1.call-update) | async-done | bytes 4194320 | tf_op jit(solution)/shard_map/all_gather | solution.py:50
  254.9 107.4 %all-gather.10.cloned.1.call-done = f32[4096,512]{1,0:T(8,128)} async-done(((f32[512,512]{1,0:T(8,128)}), f32[4096,512]{1,0:T(8,128)}) %all-gather.10.cloned.1.call-update) | async-done | bytes 8388624 | tf_op jit(solution)/shard_map/all_gather | solution.py:52
  362.3 10.6 %copy.45 = f32[4,8,128,512]{2,1,0,3:T(8,128)} copy(f32[4,8,128,512]{3,2,0,1:T(8,128)} %bitcast.151) | data formatting | bytes 16777216 | tf_op jit(solution)/shard_map/transpose | solution.py:54
  372.9 11.5 %copy.62 = f32[64,8,32,128]{3,1,2,0:T(8,128)S(1)} copy(f32[64,8,32,128]{3,2,1,0:T(8,128)} %bitcast.148) | data formatting | bytes 16777216
  389.5 11.9 %cholesky.107 = f32[128,128]{1,0:T(8,128)S(1)} custom-call(f32[128,128]{1,0:T(8,128)S(1)} %cholesky.272), custom_call_target="Cholesky" | custom-call | tf_op jit(solution)/shard_map/jit(cholesky)/cholesky | solution.py:56
  401.6 9.8 %custom-call.31 = f32[1,128,128]{1,2,0:T(8,128)S(1)} custom-call(f32[1,128,128]{2,1,0:T(8,128)S(1)} %get-tuple-element.36), custom_call_target="InvertDiagBlocksLowerTriangular" | custom-call | tf_op jit(solution)/shard_map/jit(cholesky)/cholesky | solution.py:56
  412.0 11.7 %cholesky.223 = f32[128,128]{1,0:T(8,128)S(1)} custom-call(f32[128,128]{1,0:T(8,128)S(1)} %cholesky.276), custom_call_target="Cholesky" | custom-call | tf_op jit(solution)/shard_map/jit(cholesky)/cholesky | solution.py:56
  423.8 9.8 %custom-call.32 = f32[1,128,128]{1,2,0:T(8,128)S(1)} custom-call(f32[1,128,128]{2,1,0:T(8,128)S(1)} %get-tuple-element.33), custom_call_target="InvertDiagBlocksLowerTriangular" | custom-call | tf_op jit(solution)/shard_map/jit(cholesky)/cholesky | solution.py:56
  434.3 12.1 %cholesky.244 = f32[128,128]{1,0:T(8,128)S(1)} custom-call(f32[128,128]{1,0:T(8,128)S(1)} %cholesky.281), custom_call_target="Cholesky" | custom-call | tf_op jit(solution)/shard_map/jit(cholesky)/cholesky | solution.py:56
  447.0 9.8 %custom-call.33 = f32[1,128,128]{1,2,0:T(8,128)S(1)} custom-call(f32[1,128,128]{2,1,0:T(8,128)S(1)} %get-tuple-element.30), custom_call_target="InvertDiagBlocksLowerTriangular" | custom-call | tf_op jit(solution)/shard_map/jit(cholesky)/cholesky | solution.py:56
  457.4 11.7 %cholesky.261 = f32[128,128]{1,0:T(8,128)S(1)} custom-call(f32[128,128]{1,0:T(8,128)S(1)} %convolution_subtract_fusion.4), custom_call_target="Cholesky" | custom-call | tf_op jit(solution)/shard_map/jit(cholesky)/cholesky | solution.py:56
  473.0 7.7 %while.1 = (s32[]{:T(128)}, f32[512,512]{1,0:T(8,128)S(1)}, s32[4,2]{0,1:T(2,128)S(1)}, f32[4,128,128]{2,1,0:T(8,128)S(1)}, s32[]{:T(128)}) while((s32[]{:T(128)}, f32[512,512]{1,0:T(8,128)S(1)}, s32[4,2]{0,1:T(2,128)S(1)}, f32[4,128,128]{2,1,0:T(8,128)S(1)}, s32[]{:T(128)}) %tuple.31), condition=%wide.while_cond, body=%wide.while_body.sunk | while | flops 2 | bytes 131181 | solution.py:57
  480.7 39.5 %custom-call.34 = f32[4,128,128]{1,2,0:T(8,128)S(1)} custom-call(f32[4,128,128]{2,1,0:T(8,128)S(1)} %get-tuple-element.12), custom_call_target="InvertDiagBlocksLowerTriangular" | custom-call | tf_op jit(solution)/shard_map/jit(_solve_triangular)/triangular_solve | solution.py:57
  535.2 5.7 fusion.6
  546.6 9.0 %copy.53 = f32[4096,512]{1,0:T(8,128)} copy(f32[4096,512]{0,1:T(8,128)} %maximum_bitcast_fusion) | data formatting | bytes 16777216 | tf_op jit(solution)/shard_map/reshape | solution.py:58
  (97 shorter events, 57.8 us)
Async XLA Ops:
  6.5 134.9 %copy-start = (f32[4096]{0:T(1024)S(1)}, f32[4096]{0:T(1024)}, u32[]{:S(2)}) copy-start(f32[4096]{0:T(1024)} %param.11) | copy-start | bytes 49156
  6.5 77.6 %all-gather.6.cloned.1.call-start = ((), (), s32[]{:S(2)}) async-start(), calls=%async_computation.1 | async-start | bytes 4718592 | tf_op jit(solution)/shard_map/all_gather | solution.py:26
  9.9 203.7 %reduce-scatter.2.cloned.1.call-start = ((), (), s32[]{:S(2)}) async-start(), calls=%async_computation.2 | async-start | bytes 8912896 | tf_op jit(solution)/shard_map/reduce_scatter | solution.py:41
  141.2 110.5 %all-gather.8.cloned.1.call-start = ((), (), s32[]{:S(2)}) async-start(), calls=%async_computation.3 | async-start | bytes 4456448 | tf_op jit(solution)/shard_map/all_gather | solution.py:50
  215.6 146.7 %all-gather.10.cloned.1.call-start = ((), (), s32[]{:S(2)}) async-start(), calls=%async_computation.4 | async-start | bytes 9437184 | tf_op jit(solution)/shard_map/all_gather | solution.py:52
  384.4 3.2 copy-start.2
  559.8 6.1 %copy-start.1 = (f32[4096]{0:T(1024)S(1)}, f32[4096]{0:T(1024)}, u32[]{:S(2)}) copy-start(f32[4096]{0:T(1024)} %param.11) | copy-start | bytes 49156
Sparse Core Ops, SparseCore 0:
  10.0 74.1 all-gather.5
  141.3 72.2 reduce-scatter.1
  215.7 35.8 all-gather.7
  254.9 107.3 all-gather.9
where the time goes:
time: 579 us; the launch traced here: 573 us
  waiting for transfers between devices  245 us (42%)
  other arithmetic  156 us (27%)
  local copies, waits for them, and re-layouts  79 us (14%)
  blocking collectives  43.3 us (7%)
  matrix products  32.5 us (6%)
  between operations  16.9 us (3%)
    all_gather x1, waiting for transfers between devices, body(): every = lax.all_gather(panel_here, 'row', axis=0, tiled=True)  107 us
    another operation x14, other arithmetic, body(): lower = jnp.linalg.cholesky(natural[:PW])  78.9 us
    reduce_scatter x1, waiting for transfers between devices, body(): lax.psum_scatter(partial_value, 'col', scatter_dimension=1, tiled=True)  71.5 us
    another operation x3, other arithmetic, body(): factor = jax.scipy.linalg.solve_triangular(lower, natural.T, lower=True).T  39.6 us
    all_gather x1, waiting for transfers between devices, body(): slab = lax.all_gather(owned_blocks[:, :1], 'col', axis=1, tiled=True)  36 us
    all_gather x1, waiting for transfers between devices, body(): data = lax.all_gather(cleaned, 'row', axis=0, tiled=True)  29.7 us
    scatter-add x1, other arithmetic, body(): partial_value = empty.at[row_pos[:, None], col_pos].add(product)  27.7 us
    all_gather x1, blocking collectives, body(): ids = lax.all_gather(ids_wire, 'row', axis=0, tiled=True)  24.9 us
  transfers between devices with their start and end apart: 4, of which 4 were waited for; matrix products, arithmetic and copies ran while one was open for 0% of the time, Pallas kernels for 0%

commit v1 on v0

v1 whole, which is shorter than its diff:
```python
import jax, jax.numpy as jnp
from jax import lax
from jax.sharding import PartitionSpec as P
from jax.experimental import pallas as pl
from jax.experimental.pallas import tpu as pltpu

HI = lax.Precision.HIGHEST
NA = 896


def tdot(a, b):
    return lax.dot_general(a, b, (((0,), (0,)), ((), ())), precision=HI,
                           preferred_element_type=jnp.float32)


def bc(v):
    return jnp.broadcast_to(v, (8, 128))


def eliminate(x_ref):
    sub = lax.broadcasted_iota(jnp.int32, (8, 128), 0)
    for blk in range(4):
        lo = blk * 128
        nl = (NA - lo) // 128
        for h in range(4):
            r0 = lo + 32 * h
            xs = [[x_ref[r0 + 8 * b:r0 + 8 * b + 8, lo + 128 * l:lo + 128 * l + 128] for l in range(nl)]
                  for b in range(4)]
            for j in range(4):
                lane = 32 * h + 8 * j
                cs = {b: [bc(xs[b][0][:, lane + i:lane + i + 1]) for i in range(8)] for b in range(j, 4)}
                scale = jnp.zeros((8, 128), jnp.float32)
                for i in range(8):
                    p = bc(cs[j][i][i:i + 1, :])
                    rp = 1.0 / p
                    scale = jnp.where(sub == i, lax.rsqrt(p), scale)
                    f = {b: cs[b][i] * rp for b in range(j, 4)}
                    f[j] = jnp.where(sub > i, f[j], 0.0)
                    for m in range(i + 1, 8):
                        t = bc(cs[j][m][i:i + 1, :])
                        for b in range(j, 4):
                            cs[b][m] = cs[b][m] - f[b] * t
                    for l in range(nl):
                        t = bc(xs[j][l][i:i + 1, :])
                        for b in range(j, 4):
                            xs[b][l] = xs[b][l] - f[b] * t
                for l in range(nl):
                    xs[j][l] = xs[j][l] * scale
                    x_ref[r0 + 8 * j:r0 + 8 * j + 8, lo + 128 * l:lo + 128 * l + 128] = xs[j][l]
            if h < 3:
                u = x_ref[r0:r0 + 32, lo:NA]
                t = tdot(u[:, :128], u)
                x_ref[r0 + 32:lo + 128, lo:NA] = x_ref[r0 + 32:lo + 128, lo:NA] - t[32 * (h + 1):, :]
        for nxt in range(blk + 1, 4):
            c = nxt * 128
            x_ref[c:c + 128, c:NA] = x_ref[c:c + 128, c:NA] - tdot(
                x_ref[lo:lo + 128, c:c + 128], x_ref[lo:lo + 128, c:NA])


def kernel_c(panel, own, reg, out, x_ref):
    q = lax.axis_index("col")
    r = lax.axis_index("row")
    cls = q // 4
    kr = lax.rem(r, 4)
    kc = lax.rem(q, 4)
    owner = (r // 4) == lax.rem(cls, 2)
    eye = (lax.broadcasted_iota(jnp.int32, (128, 128), 0) == lax.broadcasted_iota(jnp.int32, (128, 128), 1))
    out[...] = jnp.zeros_like(out)

    def diag(block):
        return jnp.where(eye, jnp.broadcast_to(reg[pl.ds(block, 1), :], (128, 128)), 0.0)

    def blk(t, i, j):
        return jnp.concatenate([panel[0, t, i, j], panel[1, t, i, j]], axis=0)

    def mine(t, u):
        base = jnp.concatenate([own[t, u, 0], own[t, u, 1]], axis=0)
        if t == u:
            base = base + jnp.where(kr == kc, 1.0, 0.0) * diag(cls * 4 + kr + 16 * t)
        return base

    @pl.when(owner & (cls > 0))
    def _():
        for t in range(2):
            at = pl.multiple_of((cls // 2 + 2 * t) * 128, 128)
            for u in range(2):
                out[pl.ds(at, 128), u * 128:u * 128 + 128] = mine(t, u)

    @pl.when(owner & (cls == 0))
    def _():
        for i in range(4):
            for j in range(i, 4):
                s = 0.5 * (blk(0, i, j) + blk(0, j, i).T)
                if i == j:
                    s = s + diag(i)
                x_ref[i * 128:i * 128 + 128, j * 128:j * 128 + 128] = s
        for k in range(4):
            rows = slice(k * 128, k * 128 + 128)
            x_ref[rows, 512:640] = blk(0, kr, k).T + jnp.where(kr == k, 1.0, 0.0) * diag(k)
            x_ref[rows, 640:768] = blk(1, kr, k).T
            x_ref[rows, 768:896] = blk(1, kc, k).T
        eliminate(x_ref)
        at = pl.multiple_of(kc * 128, 128)
        out[0:128, 0:128] = x_ref[pl.ds(at, 128), 512:640].T
        out[256:384, 0:128] = x_ref[pl.ds(at, 128), 640:768].T
        out[256:384, 128:256] = mine(1, 1) - tdot(x_ref[:, 640:768], x_ref[:, 768:896])


def finish(panel, own, reg):
    return pl.pallas_call(
        kernel_c,
        out_shape=jax.ShapeDtypeStruct((512, 256), jnp.float32),
        in_specs=[pl.BlockSpec(memory_space=pltpu.VMEM)] * 3,
        out_specs=pl.BlockSpec(memory_space=pltpu.VMEM),
        scratch_shapes=[pltpu.VMEM((512, NA), jnp.float32)],
        compiler_params=pltpu.CompilerParams(vmem_limit_bytes=40 * 1024 * 1024),
    )(panel, own, reg)
ROWS = 528
MESH = pl.DeviceIdType.MESH


def kernel_a(data, scale, ids, live_rows, live_blocks, own, panel,
             gat, lbuf, rbuf, part, land, res,
             w1s, w1f, w1r, w2s, w2r, w3s, panel_r, own_r, sib_s, sib_r):
    r = lax.axis_index("row")
    q = lax.axis_index("col")
    z, yh = r // 2, lax.rem(r, 2)
    zh, zl = z // 2, lax.rem(z, 2)
    yl, j = q // 8, lax.rem(q, 8)
    x, e = j // 2, lax.rem(j, 2)
    xh, xl = x // 2, lax.rem(x, 2)
    pos = 2 * r + yl
    cls = 2 * yl + xh
    sibling = (r, q + 1 - 2 * e)

    def ring(d):
        x2 = lax.rem(x + d, 4)
        return (r, yl * 8 + 2 * x2 + e), 2 * x2 + e

    def plane(p):
        return (p // 2, lax.rem(p, 2) * 8 + j)

    barrier = pltpu.get_barrier_semaphore()
    for d in range(1, 4):
        pl.semaphore_signal(barrier, inc=1, device_id=ring(d)[0], device_id_type=MESH)
    pl.semaphore_signal(barrier, inc=1, device_id=sibling, device_id_type=MESH)
    for d in range(1, 16):
        pl.semaphore_signal(barrier, inc=1, device_id=plane(lax.rem(pos + d, 16)), device_id_type=MESH)

    def prepare(s):
        row = lax.broadcasted_iota(jnp.int32, (16, 128), 0)
        on = s < live_blocks[0]
        meta = jnp.where(row == 0, jnp.broadcast_to(scale[...].astype(jnp.float32)[s:s + 1, :], (16, 128)), 0.0)
        for k in range(4):
            keep = jnp.where(on & (k < live_rows[s]), 1.0, 0.0)
            gat[s, j, k * 128:k * 128 + 128, :] = (data[s, k].astype(jnp.float32) * keep).astype(jnp.bfloat16)
            late = jnp.where(ids[s, k] >= 16, 1.0, 0.0)
            meta = jnp.where(row == k + 1, late, meta)
        gat[s, j, 512:528, :] = meta.astype(jnp.bfloat16)

    def w1_copy(s, d):
        target = sibling if d == 0 else ring(d)[0]
        return pltpu.make_async_remote_copy(
            src_ref=gat.at[s, j], dst_ref=gat.at[s, j], send_sem=w1s.at[s, d], recv_sem=w1r.at[s, j],
            device_id=target, device_id_type=MESH)

    def forward_copy(s, d):
        j2 = ring(d)[1]
        return pltpu.make_async_remote_copy(
            src_ref=gat.at[s, j2], dst_ref=gat.at[s, j2], send_sem=w1f.at[s, d - 1], recv_sem=w1r.at[s, j2],
            device_id=sibling, device_id_type=MESH)

    def w1_arrived(s, j2):
        pltpu.make_async_remote_copy(
            src_ref=gat.at[s, j2], dst_ref=gat.at[s, j2], send_sem=w1f.at[s, 0], recv_sem=w1r.at[s, j2],
            device_id=sibling, device_id_type=MESH).wait_recv()

    def w2_copy(s, d):
        to = lax.rem(pos + d, 16)
        return pltpu.make_async_remote_copy(
            src_ref=part.at[s, to], dst_ref=land.at[s, pos], send_sem=w2s.at[s, d - 1], recv_sem=w2r.at[s, pos],
            device_id=plane(to), device_id_type=MESH)

    def w2_arrived(s, src):
        pltpu.make_async_remote_copy(
            src_ref=part.at[s, src], dst_ref=land.at[s, src], send_sem=w2s.at[s, 0], recv_sem=w2r.at[s, src],
            device_id=plane(src), device_id_type=MESH).wait_recv()

    def forward(s):
        for d in (1, 3, 2):
            w1_arrived(s, ring(d)[1])
            forward_copy(s, d).start()

    def compute(s):
        w1_arrived(s, 2 * x + 1 - e)
        for d in (1, 3, 2):
            w1_arrived(s, 2 * lax.rem(x + d, 4) + 1 - e)

        def build(c, _):
            meta = gat[s, c, 512:528, :].astype(jnp.float32)
            sc = meta[0:1, :]
            at = pl.multiple_of(c * 128, 128)
            for k in range(2):
                t = jnp.where(xh == 0, meta[1 + k:2 + k, :], meta[3 + k:4 + k, :])
                a = gat[s, c, pl.ds(pl.multiple_of((2 * xh + k) * 128, 128), 128), :].astype(jnp.float32)
                g = (a * sc).astype(jnp.bfloat16).astype(jnp.float32)
                lbuf[2 * k * 128:2 * k * 128 + 128, pl.ds(at, 128)] = (g * (1.0 - t)).astype(jnp.bfloat16)
                lbuf[2 * k * 128 + 128:2 * k * 128 + 256, pl.ds(at, 128)] = (g * t).astype(jnp.bfloat16)
            t0 = jnp.where(e == 0, meta[1:2, :], meta[2:3, :])
            t1 = jnp.where(e == 0, meta[3:4, :], meta[4:5, :])
            t = jnp.where(xl == 0, t0, t1)
            a = gat[s, c, pl.ds(pl.multiple_of((2 * xl + e) * 128, 128), 128), :].astype(jnp.float32)
            rbuf[0:128, pl.ds(at, 128)] = (a * (1.0 - t)).astype(jnp.bfloat16)
            rbuf[128:256, pl.ds(at, 128)] = (a * t).astype(jnp.bfloat16)
            return 0

        lax.fori_loop(0, 8, build, 0)
        for k in range(2):
            for t in range(2):
                row = (2 * k + t) * 128
                acc = lax.dot_general(lbuf[row:row + 128, :], rbuf[...], (((1,), (1,)), ((), ())),
                                      preferred_element_type=jnp.float32)
                for half in range(2):
                    for u in range(2):
                        part[s, t * 8 + half * 4 + k * 2 + u] = acc[half * 64:half * 64 + 64, u * 128:u * 128 + 128]

    def panel_copy(d):
        xd, yd, zd = d % 2, (d // 2) % 2, d // 4
        to = (zd * 2 + yd, xd * 2 + zl)
        kr, kc = 2 * xh + yh, 2 * xl + e
        copy = pltpu.make_async_remote_copy(
            src_ref=res.at[0], dst_ref=panel.at[zl, zh, kr, kc], send_sem=w3s.at[0, d],
            recv_sem=panel_r.at[zh, kr, kc], device_id=to, device_id_type=MESH)
        return copy, (to[0] != r) | (to[1] != q)

    def own_copy(s):
        sh, sl = s // 2, lax.rem(s, 2)
        to = ((2 * sl + xh) * 2 + yh, sh * 8 + (2 * sl + xl) * 2 + e)
        copy = pltpu.make_async_remote_copy(
            src_ref=res.at[s], dst_ref=own.at[zh, yl, zl], send_sem=w3s.at[s, 0],
            recv_sem=own_r.at[zh, yl, zl], device_id=to, device_id_type=MESH)
        return copy, (to[0] != r) | (to[1] != q)

    def finish_sum(s):
        for d in range(1, 16):
            w2_arrived(s, lax.rem(pos + d, 16))
        total = part[s, pos]
        for d in range(1, 16):
            total = total + land[s, lax.rem(pos + d, 16)]
        res[s] = total

        @pl.when(s == 0)
        def _():
            @pl.when(yl == 0)
            def _():
                for d in range(8):
                    copy, remote = panel_copy(d)
                    pl.when(remote)(copy.start)

                @pl.when((cls == 0) & (zh == 0) & (zl == e))
                def _():
                    panel[zl, 0, yh, 2 * xl + e] = total

            @pl.when((yl == 1) & (zh == 1))
            def _():
                own_copy(s)[0].start()

        @pl.when(s > 0)
        def _():
            copy, remote = own_copy(s)
            pl.when(remote)(copy.start)

            @pl.when(jnp.logical_not(remote))
            def _():
                own[zh, yl, zl] = total

    prepare(0)
    pl.semaphore_wait(barrier, 19)
    for d in (1, 3, 2, 0):
        w1_copy(0, d).start()

    for s in range(1, 4):
        prepare(s)
        for d in (1, 3, 2, 0):
            w1_copy(s, d).start()
    forward(0)

    def step(s, _):
        compute(s)
        for d in range(1, 16):
            w2_copy(s, d).start()

        @pl.when(s < 3)
        def _():
            forward(s + 1)

        finish_sum(s)
        return 0

    lax.fori_loop(0, 4, step, 0)

    @pl.when((cls == 0) & (zh == 0))
    def _():
        for t in range(2):
            def arrived(i, _):
                a, b = i // 4, lax.rem(i, 4)
                here = (t == 0) & (a == yh) & (b == 2 * xl + e) & (zl == e)

                @pl.when(jnp.logical_not(here))
                def _():
                    pltpu.make_async_remote_copy(
                        src_ref=res.at[0], dst_ref=panel.at[e, t, a, b], send_sem=w3s.at[0, 0],
                        recv_sem=panel_r.at[t, a, b], device_id=sibling, device_id_type=MESH).wait_recv()
                return 0

            lax.fori_loop(0, 16, arrived, 0)
            pltpu.make_async_remote_copy(
                src_ref=panel.at[e, t], dst_ref=panel.at[e, t], send_sem=sib_s.at[t], recv_sem=sib_r.at[t],
                device_id=sibling, device_id_type=MESH).start()
        for t in range(2):
            copy = pltpu.make_async_remote_copy(
                src_ref=panel.at[e, t], dst_ref=panel.at[1 - e, t], send_sem=sib_s.at[t], recv_sem=sib_r.at[t],
                device_id=sibling, device_id_type=MESH)
            copy.wait_recv()
            copy.wait_send()

    @pl.when(zh == xh)
    def _():
        for t in range(2):
            for u in range(2):
                for half in range(2):
                    here = (xh == zl) & (yl == u) & (zh == t) & (zl == half)
                    wanted = ((cls > 0) & jnp.logical_not(here)) | ((cls == 0) & (t == 1) & (u == 1))

                    @pl.when(wanted)
                    def _():
                        pltpu.make_async_remote_copy(
                            src_ref=res.at[0], dst_ref=own.at[t, u, half], send_sem=w3s.at[0, 0],
                            recv_sem=own_r.at[t, u, half], device_id=sibling, device_id_type=MESH).wait_recv()

    def sent(s, _):
        for d in range(4):
            w1_copy(s, d).wait_send()
        for d in range(1, 4):
            forward_copy(s, d).wait_send()
        for d in range(1, 16):
            w2_copy(s, d).wait_send()

        @pl.when(s > 0)
        def _():
            copy, remote = own_copy(s)
            pl.when(remote)(copy.wait_send)
        return 0

    lax.fori_loop(0, 4, sent, 0)

    @pl.when(yl == 0)
    def _():
        for d in range(8):
            copy, remote = panel_copy(d)
            pl.when(remote)(copy.wait_send)

    @pl.when((yl == 1) & (zh == 1))
    def _():
        own_copy(0)[0].wait_send()


def assemble(data, scale, ids, live_rows, live_blocks):
    vmem = pl.BlockSpec(memory_space=pltpu.VMEM)
    smem = pl.BlockSpec(memory_space=pltpu.SMEM)
    dma = pltpu.SemaphoreType.DMA
    return pl.pallas_call(
        kernel_a,
        out_shape=(jax.ShapeDtypeStruct((2, 2, 2, 64, 128), jnp.float32),
                   jax.ShapeDtypeStruct((2, 2, 4, 4, 64, 128), jnp.float32)),
        in_specs=[vmem, vmem, smem, smem, smem],
        out_specs=(vmem, vmem),
        scratch_shapes=[
            pltpu.VMEM((4, 8, ROWS, 128), jnp.bfloat16),
            pltpu.VMEM((512, 1024), jnp.bfloat16),
            pltpu.VMEM((256, 1024), jnp.bfloat16),
            pltpu.VMEM((4, 16, 64, 128), jnp.float32),
            pltpu.VMEM((4, 16, 64, 128), jnp.float32),
            pltpu.VMEM((4, 64, 128), jnp.float32),
            dma((4, 4)), dma((4, 3)), dma((4, 8)), dma((4, 15)), dma((4, 16)), dma((4, 8)),
            dma((2, 4, 4)), dma((2, 2, 2)), dma((2,)), dma((2,)),
        ],
        compiler_params=pltpu.CompilerParams(
            collective_id=0, has_side_effects=True, vmem_limit_bytes=40 * 1024 * 1024),
    )(data, scale, ids, live_rows, live_blocks)


def body(col_data, col_scale, row_ids, live_rows, live_blocks, row_reg):
    own, panel = assemble(col_data, col_scale, row_ids, live_rows, live_blocks)
    return finish(panel, own, row_reg.reshape(32, 128))


def solution(mesh):
    return jax.shard_map(
        body,
        mesh=mesh,
        in_specs=(
            P(("row", "col"), None, None, None),
            P(("row", "col"), None),
            P(("row", "col"), None),
            P(("row", "col")),
            P(("row", "col")),
            P(),
        ),
        out_specs=P("row", "col"),
        check_vma=False,
    )
```

time: 579 us -> 101 us (0.17)
  waiting for transfers between devices: 245 us -> 0 us
  other arithmetic: 156 us -> 0 us
  Pallas kernels: 0 us -> 94.6 us
  local copies, waits for them, and re-layouts: 79 us -> 3.76 us
  blocking collectives: 43.3 us -> 0 us
  matrix products: 32.5 us -> 0 us
  between operations: 16.9 us -> 0.68 us
    all_gather x3 -> x0, waiting for transfers between devices: 173 us -> none  [the longest x1 107 us: body(): every = lax.all_gather(panel_here, 'row', axis=0, tiled=True)]
    another operation x17 -> x0, other arithmetic: 119 us -> none  [the longest x14 78.9 us: body(): lower = jnp.linalg.cholesky(natural[:PW])]
    pallas_call x0 -> x2, Pallas kernels: none -> 94.6 us  [the longest x1 74.4 us: assemble(): pl.pallas_call(kernel_a, out_shape=(jax.ShapeDtypeStruct((2, 2, 2, 64, 12...]
    reduce_scatter x1 -> x0, waiting for transfers between devices: 71.5 us -> none  [body(): lax.psum_scatter(partial_value, 'col', scatter_dimension=1, tiled=True)]
    all_gather x2 -> x0, blocking collectives: 43.3 us -> none  [the longest x1 24.9 us: body(): ids = lax.all_gather(ids_wire, 'row', axis=0, tiled=True)]
    scatter-add x1 -> x0, other arithmetic: 27.7 us -> none  [body(): partial_value = empty.at[row_pos[:, None], col_pos].add(product)]
    another operation x13 -> x0, matrix products: 24.4 us -> none  [the longest x7 22.5 us: body(): factor = jax.scipy.linalg.solve_triangular(lower, natural.T, lower=True).T]
    transpose x5 -> x0, local copies, waits for them, and re-layouts: 21.8 us -> none  [the longest x1 10.6 us: body(): every.reshape(nrow, nbl_here, height, PW).transpose(1, 0, 2, 3)]
  transfers between devices with their start and end apart: 4 -> 0, of which waited for: 4 -> 0; matrix products, arithmetic and copies ran while one was open for 0% -> 0% of each run, Pallas kernels for 0% -> 0%
where the time goes in v1:
time: 101 us; the launch traced here: 99 us
  Pallas kernels  94.6 us (94%)
  local copies, waits for them, and re-layouts  3.76 us (4%)
    pallas_call x1, Pallas kernels, assemble(): pl.pallas_call(kernel_a, out_shape=(jax.ShapeDtypeStruct((2, 2, 2, 64, 12...  74.4 us
    pallas_call x1, Pallas kernels, finish(): pl.pallas_call(kernel_c, out_shape=jax.ShapeDtypeStruct((512, 256), jnp.f...  20.2 us
    unnamed x10, local copies, waits for them, and re-layouts  3.76 us

profile of v1, /device:TPU:0, one launch (start us, length us, event | category | flops | bytes accessed | tf_op | source)
XLA Modules:
  0.0 99.0 jit_solution(1561929845385939774)
XLA Ops:
  0.7 0.0 copy-start
  0.7 1.0 %copy-done = bf16[4,4,128,128]{3,2,1,0:T(8,128)(2,1)S(1)} copy-done((bf16[4,4,128,128]{3,2,1,0:T(8,128)(2,1)S(1)}, bf16[4,4,128,128]{3,2,1,0:T(8,128)(2,1)}, u32[]{:S(2)}) %copy-start) | copy-done | bytes 524312
  1.7 0.0 copy-start.2
  1.7 0.7 copy-done.2
  2.4 0.0 copy-start.3
  2.4 0.7 copy-done.3
  3.1 0.0 copy-start.4
  3.1 0.7 copy-done.4
  3.7 74.4 %shard_map.64 = (f32[2,2,2,64,128]{4,3,2,1,0:T(8,128)S(1)}, f32[2,2,4,4,64,128]{5,4,3,2,1,0:T(8,128)S(1)}) custom-call(bf16[4,4,128,128]{3,2,1,0:T(8,128)(2,1)S(1)} %copy-done, bf16[4,128]{1,0:T(4,128)(2,1)S(1)} %copy-done.3, s32[4,4]{1,0:T(4,128)S(1)} %copy-done.2, s32[4]{0:T(128)S(1)} %copy-done.4, s32[1]{0:T(128)S(6)} %copy.7.live_blocks), custom_call_target="tpu_custom_call" | custom-call | tf_op jit(solution)/shard_map/pallas_call | solution.py:372
  78.1 0.0 copy-start.1
  78.1 0.7 copy-done.1
  78.8 20.2 %shard_map.65 = f32[512,256]{1,0:T(8,128)} custom-call(f32[2,2,4,4,64,128]{5,4,3,2,1,0:T(8,128)S(1)} %get-tuple-element.7.panel, f32[2,2,2,64,128]{4,3,2,1,0:T(8,128)S(1)} %get-tuple-element.8.own, f32[32,128]{1,0:T(8,128)S(1)} %bitcast.1), custom_call_target="tpu_custom_call" | custom-call | tf_op jit(solution)/shard_map/pallas_call | solution.py:110
Async XLA Ops:
  0.7 1.0 %copy-start = (bf16[4,4,128,128]{3,2,1,0:T(8,128)(2,1)S(1)}, bf16[4,4,128,128]{3,2,1,0:T(8,128)(2,1)}, u32[]{:S(2)}) copy-start(bf16[4,4,128,128]{3,2,1,0:T(8,128)(2,1)} %data.1) | copy-start | bytes 1572868
  1.7 0.7 copy-start.2
  2.4 0.7 copy-start.3
  3.1 0.7 copy-start.4
  78.1 0.7 copy-start.1

commit v2 on v1

v2 whole, which is shorter than its diff:
```python
import jax
import jax.numpy as jnp
from jax import lax
from jax.experimental import pallas as pl
from jax.experimental.pallas import tpu as pltpu
from jax.sharding import PartitionSpec as P

HI = lax.Precision.HIGHEST
NA = 896
ROWS = 528
MESH = pl.DeviceIdType.MESH


def tdot(a, b):
    return lax.dot_general(a, b, (((0,), (0,)), ((), ())), precision=HI,
                           preferred_element_type=jnp.float32)


def fdot(a, b):
    return jnp.dot(a, b, precision=HI, preferred_element_type=jnp.float32)


def lanes(v):
    return jnp.broadcast_to(v, (v.shape[0], 128))


def diag_factor(d, between=None):
    row8 = lax.broadcasted_iota(jnp.int32, (8, 128), 0)
    e = jnp.where(lax.broadcasted_iota(jnp.int32, (128, 128), 0) == lax.broadcasted_iota(jnp.int32, (128, 128), 1), 1.0, 0.0)
    us, es = [], []
    for h in range(4):
        x, y = d[:32], e[:32]
        done_x, done_y = [], []
        for j in range(4):
            lane = 32 * h + 8 * j
            rows = 32 - 8 * j
            row = lax.broadcasted_iota(jnp.int32, (rows, 128), 0)
            cs = [lanes(x[:, lane + i:lane + i + 1]) for i in range(8)]
            scale = jnp.zeros((8, 128), jnp.float32)
            for i in range(8):
                p = cs[i][i:i + 1, :]
                rp = 1.0 / p
                scale = jnp.where(row8 == i, lax.rsqrt(p), scale)
                f = jnp.where(row > i, cs[i] * rp, 0.0)
                for m in range(i + 1, 8):
                    cs[m] = cs[m] - f * cs[m][i:i + 1, :]
                x = x - f * x[i:i + 1, :]
                y = y - f * y[i:i + 1, :]
            done_x.append(x[:8] * scale)
            done_y.append(y[:8] * scale)
            x, y = x[8:], y[8:]
        ux = jnp.concatenate(done_x, axis=0)
        uy = jnp.concatenate(done_y, axis=0)
        us.append(ux)
        es.append(uy)
        if h < 3:
            n = 128 - 32 * (h + 1)
            left = ux[:, :]
            d = d[32:] - tdot(left, ux)[32 * (h + 1):]
            e = e[32:] - tdot(left, uy)[32 * (h + 1):]
    return jnp.concatenate(us, axis=0), jnp.concatenate(es, axis=0)


def kernel(data_h, scale_h, ids_h, live_rows_h, live_blocks_h, reg_h, out,
           data, scale, ids, live_rows, live_blocks, reg, own, panel,
           gat, lbuf, rbuf, part, land, res, x_ref,
           ins, w1s, w1f, w1r, w2s, w2r, w3s, panel_r, own_r, sib_s, sib_r):
    loads = [pltpu.make_async_copy(a, b, ins.at[i]) for i, (a, b) in enumerate((
        (ids_h, ids), (live_rows_h, live_rows), (live_blocks_h, live_blocks), (scale_h, scale),
        (data_h.at[0], data.at[0]), (data_h.at[1], data.at[1]), (data_h.at[2], data.at[2]),
        (data_h.at[3], data.at[3]), (reg_h, reg)))]
    for load in loads:
        load.start()
    r = lax.axis_index("row")
    q = lax.axis_index("col")
    z, yh = r // 2, lax.rem(r, 2)
    zh, zl = z // 2, lax.rem(z, 2)
    yl, j = q // 8, lax.rem(q, 8)
    x, e = j // 2, lax.rem(j, 2)
    xh, xl = x // 2, lax.rem(x, 2)
    pos = 2 * r + yl
    cls = 2 * yl + xh
    sibling = (r, q + 1 - 2 * e)

    def ring(d):
        x2 = lax.rem(x + d, 4)
        return (r, yl * 8 + 2 * x2 + e), 2 * x2 + e

    def plane(p):
        return (p // 2, lax.rem(p, 2) * 8 + j)

    barrier = pltpu.get_barrier_semaphore()
    for d in range(1, 4):
        pl.semaphore_signal(barrier, inc=1, device_id=ring(d)[0], device_id_type=MESH)
    pl.semaphore_signal(barrier, inc=1, device_id=sibling, device_id_type=MESH)
    for d in range(1, 16):
        pl.semaphore_signal(barrier, inc=1, device_id=plane(lax.rem(pos + d, 16)), device_id_type=MESH)

    def prepare(s):
        row = lax.broadcasted_iota(jnp.int32, (16, 128), 0)
        on = s < live_blocks[0]
        meta = jnp.where(row == 0, jnp.broadcast_to(scale[...].astype(jnp.float32)[s:s + 1, :], (16, 128)), 0.0)
        for k in range(4):
            keep = jnp.where(on & (k < live_rows[s]), 1.0, 0.0)
            gat[s, j, k * 128:k * 128 + 128, :] = (data[s, k].astype(jnp.float32) * keep).astype(jnp.bfloat16)
            late = jnp.where(ids[s, k] >= 16, 1.0, 0.0)
            meta = jnp.where(row == k + 1, late, meta)
        gat[s, j, 512:528, :] = meta.astype(jnp.bfloat16)

    def w1_copy(s, d):
        target = sibling if d == 0 else ring(d)[0]
        return pltpu.make_async_remote_copy(
            src_ref=gat.at[s, j], dst_ref=gat.at[s, j], send_sem=w1s.at[s, d], recv_sem=w1r.at[s, j],
            device_id=target, device_id_type=MESH)

    def forward_copy(s, d):
        j2 = ring(d)[1]
        return pltpu.make_async_remote_copy(
            src_ref=gat.at[s, j2], dst_ref=gat.at[s, j2], send_sem=w1f.at[s, d - 1], recv_sem=w1r.at[s, j2],
            device_id=sibling, device_id_type=MESH)

    def w1_arrived(s, j2):
        pltpu.make_async_remote_copy(
            src_ref=gat.at[s, j2], dst_ref=gat.at[s, j2], send_sem=w1f.at[s, 0], recv_sem=w1r.at[s, j2],
            device_id=sibling, device_id_type=MESH).wait_recv()

    def w2_copy(s, d):
        to = lax.rem(pos + d, 16)
        return pltpu.make_async_remote_copy(
            src_ref=part.at[s, to], dst_ref=land.at[s, pos], send_sem=w2s.at[s, d - 1], recv_sem=w2r.at[s, pos],
            device_id=plane(to), device_id_type=MESH)

    def w2_arrived(s, src):
        pltpu.make_async_remote_copy(
            src_ref=part.at[s, src], dst_ref=land.at[s, src], send_sem=w2s.at[s, 0], recv_sem=w2r.at[s, src],
            device_id=plane(src), device_id_type=MESH).wait_recv()

    def forward(s):
        for d in (1, 3, 2):
            w1_arrived(s, ring(d)[1])
            forward_copy(s, d).start()

    def compute(s):
        w1_arrived(s, 2 * x + 1 - e)
        for d in (1, 3, 2):
            w1_arrived(s, 2 * lax.rem(x + d, 4) + 1 - e)

        def build(c, _):
            meta = gat[s, c, 512:528, :].astype(jnp.float32)
            sc = meta[0:1, :]
            at = pl.multiple_of(c * 128, 128)
            for k in range(2):
                t = jnp.where(xh == 0, meta[1 + k:2 + k, :], meta[3 + k:4 + k, :])
                a = gat[s, c, pl.ds(pl.multiple_of((2 * xh + k) * 128, 128), 128), :].astype(jnp.float32)
                g = (a * sc).astype(jnp.bfloat16).astype(jnp.float32)
                lbuf[2 * k * 128:2 * k * 128 + 128, pl.ds(at, 128)] = (g * (1.0 - t)).astype(jnp.bfloat16)
                lbuf[2 * k * 128 + 128:2 * k * 128 + 256, pl.ds(at, 128)] = (g * t).astype(jnp.bfloat16)
            t0 = jnp.where(e == 0, meta[1:2, :], meta[2:3, :])
            t1 = jnp.where(e == 0, meta[3:4, :], meta[4:5, :])
            t = jnp.where(xl == 0, t0, t1)
            a = gat[s, c, pl.ds(pl.multiple_of((2 * xl + e) * 128, 128), 128), :].astype(jnp.float32)
            rbuf[0:128, pl.ds(at, 128)] = (a * (1.0 - t)).astype(jnp.bfloat16)
            rbuf[128:256, pl.ds(at, 128)] = (a * t).astype(jnp.bfloat16)
            return 0

        lax.fori_loop(0, 8, build, 0)
        for k in range(2):
            for t in range(2):
                row = (2 * k + t) * 128
                acc = lax.dot_general(lbuf[row:row + 128, :], rbuf[...], (((1,), (1,)), ((), ())),
                                      preferred_element_type=jnp.float32)
                for half in range(2):
                    for u in range(2):
                        part[s, t * 8 + half * 4 + k * 2 + u] = acc[half * 64:half * 64 + 64, u * 128:u * 128 + 128]

    def panel_copy(d):
        xd, yd, zd = d % 2, (d // 2) % 2, d // 4
        to = (zd * 2 + yd, xd * 2 + zl)
        kr, kc = 2 * xh + yh, 2 * xl + e
        copy = pltpu.make_async_remote_copy(
            src_ref=res.at[0], dst_ref=panel.at[zl, zh, kr, kc], send_sem=w3s.at[0, d],
            recv_sem=panel_r.at[zh, kr, kc], device_id=to, device_id_type=MESH)
        return copy, (to[0] != r) | (to[1] != q)

    def own_copy(s):
        sh, sl = s // 2, lax.rem(s, 2)
        to = ((2 * sl + xh) * 2 + yh, sh * 8 + (2 * sl + xl) * 2 + e)
        copy = pltpu.make_async_remote_copy(
            src_ref=res.at[s], dst_ref=own.at[zh, yl, zl], send_sem=w3s.at[s, 0],
            recv_sem=own_r.at[zh, yl, zl], device_id=to, device_id_type=MESH)
        return copy, (to[0] != r) | (to[1] != q)

    def finish_sum(s):
        for d in range(1, 16):
            w2_arrived(s, lax.rem(pos + d, 16))
        total = part[s, pos]
        for d in range(1, 16):
            total = total + land[s, lax.rem(pos + d, 16)]
        res[s] = total

        @pl.when(s == 0)
        def _():
            @pl.when(yl == 0)
            def _():
                for d in range(8):
                    copy, remote = panel_copy(d)
                    pl.when(remote)(copy.start)

                @pl.when((cls == 0) & (zh == 0) & (zl == e))
                def _():
                    panel[zl, 0, yh, 2 * xl + e] = total

            @pl.when((yl == 1) & (zh == 1))
            def _():
                own_copy(s)[0].start()

        @pl.when(s > 0)
        def _():
            copy, remote = own_copy(s)
            pl.when(remote)(copy.start)

            @pl.when(jnp.logical_not(remote))
            def _():
                own[zh, yl, zl] = total

    eye = (lax.broadcasted_iota(jnp.int32, (128, 128), 0) == lax.broadcasted_iota(jnp.int32, (128, 128), 1))
    kr, kc = lax.rem(r, 4), lax.rem(q, 4)

    def diag(block):
        return jnp.where(eye, jnp.broadcast_to(reg[pl.ds(block, 1), :], (128, 128)), 0.0)

    def blk(t, a, b):
        return jnp.concatenate([panel[0, t, a, b], panel[1, t, a, b]], axis=0)

    def mine(t, u):
        base = jnp.concatenate([own[t, u, 0], own[t, u, 1]], axis=0)
        if t == u:
            base = base + jnp.where(kr == kc, 1.0, 0.0) * diag(cls * 4 + kr + 16 * t)
        return base

    def panel_half(t):
        def arrived(i, _):
            a, b = i // 4, lax.rem(i, 4)
            here = (t == 0) & (a == yh) & (b == 2 * xl + e) & (zl == e)

            @pl.when(jnp.logical_not(here))
            def _():
                pltpu.make_async_remote_copy(
                    src_ref=res.at[0], dst_ref=panel.at[e, t, a, b], send_sem=w3s.at[0, 0],
                    recv_sem=panel_r.at[t, a, b], device_id=sibling, device_id_type=MESH).wait_recv()
            return 0

        lax.fori_loop(0, 16, arrived, 0)
        pltpu.make_async_remote_copy(
            src_ref=panel.at[e, t], dst_ref=panel.at[e, t], send_sem=sib_s.at[t], recv_sem=sib_r.at[t],
            device_id=sibling, device_id_type=MESH).start()

    def panel_rest(t):
        copy = pltpu.make_async_remote_copy(
            src_ref=panel.at[e, t], dst_ref=panel.at[1 - e, t], send_sem=sib_s.at[t], recv_sem=sib_r.at[t],
            device_id=sibling, device_id_type=MESH)
        copy.wait_recv()
        copy.wait_send()

    def own_wait(t, u, half):
        pltpu.make_async_remote_copy(
            src_ref=res.at[0], dst_ref=own.at[t, u, half], send_sem=w3s.at[0, 0],
            recv_sem=own_r.at[t, u, half], device_id=sibling, device_id_type=MESH).wait_recv()

    def factor():
        panel_half(0)
        panel_rest(0)
        for i in range(4):
            for k in range(i, 4):
                s = 0.5 * (blk(0, i, k) + blk(0, k, i).T)
                if i == k:
                    s = s + diag(i)
                x_ref[i * 128:i * 128 + 128, k * 128:k * 128 + 128] = s
            x_ref[i * 128:i * 128 + 128, 512:640] = blk(0, kr, i).T + jnp.where(kr == i, 1.0, 0.0) * diag(i)
        first = None
        for n in range(4):
            lo, hi = n * 128, n * 128 + 128
            width = 640 if n == 0 else NA
            ud, li = diag_factor(x_ref[lo:hi, lo:hi])
            if n == 0:
                first = li
                panel_half(1)
            if n == 1:
                panel_rest(1)
                for k in range(4):
                    x_ref[k * 128:k * 128 + 128, 640:768] = blk(1, kr, k).T
                    x_ref[k * 128:k * 128 + 128, 768:896] = blk(1, kc, k).T
                u = fdot(first, x_ref[0:128, 640:NA])
                x_ref[0:128, 640:NA] = u
                x_ref[128:512, 640:NA] = x_ref[128:512, 640:NA] - tdot(x_ref[0:128, 128:512], u)
            u = fdot(li, x_ref[lo:hi, hi:width])
            x_ref[lo:hi, hi:width] = u
            for nxt in range(n + 1, 4):
                c = nxt * 128
                x_ref[c:c + 128, c:width] = x_ref[c:c + 128, c:width] - tdot(u[:, c - hi:c - hi + 128], u[:, c - hi:])
            if n == 2:
                finish_sum(1)
            if n == 3:
                finish_sum(2)
                finish_sum(3)
        at = pl.multiple_of(kc * 128, 128)
        out[0:128, 0:128] = x_ref[pl.ds(at, 128), 512:640].T
        out[256:384, 0:128] = x_ref[pl.ds(at, 128), 640:768].T
        left = tdot(x_ref[:, 640:768], x_ref[:, 768:896])
        for half in range(2):
            own_wait(1, 1, half)
        out[256:384, 128:256] = mine(1, 1) - left

    def send_w1(s):
        for d in (1, 3, 2, 0):
            w1_copy(s, d).start()

    def send_w2(s):
        for d in range(1, 16):
            w2_copy(s, d).start()

    for i in range(5):
        loads[i].wait()
    prepare(0)
    pl.semaphore_wait(barrier, 19)
    send_w1(0)
    for s in range(1, 4):
        loads[s + 4].wait()
        prepare(s)
    loads[8].wait()
    out[...] = jnp.zeros_like(out)
    forward(0)
    send_w1(1)
    compute(0)
    send_w2(0)
    forward(1)
    send_w1(2)
    finish_sum(0)
    compute(1)
    send_w2(1)
    forward(2)
    send_w1(3)
    compute(2)
    send_w2(2)
    forward(3)
    compute(3)
    send_w2(3)

    first_owner = (cls == 0) & (zh == 0)
    pl.when(first_owner)(factor)

    @pl.when(jnp.logical_not(first_owner))
    def _():
        for s in range(1, 4):
            finish_sum(s)

    @pl.when((cls > 0) & (zh == xh))
    def _():
        for t in range(2):
            for u in range(2):
                for half in range(2):
                    here = (xh == zl) & (yl == u) & (zh == t) & (zl == half)
                    pl.when(jnp.logical_not(here))(lambda t=t, u=u, half=half: own_wait(t, u, half))
        for t in range(2):
            at = pl.multiple_of((cls // 2 + 2 * t) * 128, 128)
            for u in range(2):
                out[pl.ds(at, 128), u * 128:u * 128 + 128] = mine(t, u)

    def sent(s, _):
        for d in range(4):
            w1_copy(s, d).wait_send()
        for d in range(1, 4):
            forward_copy(s, d).wait_send()
        for d in range(1, 16):
            w2_copy(s, d).wait_send()

        @pl.when(s > 0)
        def _():
            copy, remote = own_copy(s)
            pl.when(remote)(copy.wait_send)
        return 0

    lax.fori_loop(0, 4, sent, 0)

    @pl.when(yl == 0)
    def _():
        for d in range(8):
            copy, remote = panel_copy(d)
            pl.when(remote)(copy.wait_send)

    @pl.when((yl == 1) & (zh == 1))
    def _():
        own_copy(0)[0].wait_send()


def body(col_data, col_scale, row_ids, live_rows, live_blocks, row_reg):
    anywhere = pl.BlockSpec(memory_space=pl.ANY)
    dma = pltpu.SemaphoreType.DMA
    return pl.pallas_call(
        kernel,
        out_shape=jax.ShapeDtypeStruct((512, 256), jnp.float32),
        in_specs=[anywhere] * 6,
        out_specs=pl.BlockSpec(memory_space=pltpu.VMEM),
        scratch_shapes=[
            pltpu.VMEM((4, 4, 128, 128), jnp.bfloat16),
            pltpu.VMEM((4, 128), jnp.bfloat16),
            pltpu.SMEM((4, 4), jnp.int32),
            pltpu.SMEM((4,), jnp.int32),
            pltpu.SMEM((1,), jnp.int32),
            pltpu.VMEM((32, 128), jnp.float32),
            pltpu.VMEM((2, 2, 2, 64, 128), jnp.float32),
            pltpu.VMEM((2, 2, 4, 4, 64, 128), jnp.float32),
            pltpu.VMEM((4, 8, ROWS, 128), jnp.bfloat16),
            pltpu.VMEM((512, 1024), jnp.bfloat16),
            pltpu.VMEM((256, 1024), jnp.bfloat16),
            pltpu.VMEM((4, 16, 64, 128), jnp.float32),
            pltpu.VMEM((4, 16, 64, 128), jnp.float32),
            pltpu.VMEM((4, 64, 128), jnp.float32),
            pltpu.VMEM((512, NA), jnp.float32),
            dma((9,)),
            dma((4, 4)), dma((4, 3)), dma((4, 8)), dma((4, 15)), dma((4, 16)), dma((4, 8)),
            dma((2, 4, 4)), dma((2, 2, 2)), dma((2,)), dma((2,)),
        ],
        compiler_params=pltpu.CompilerParams(
            collective_id=0, has_side_effects=True, vmem_limit_bytes=60 * 1024 * 1024),
    )(col_data, col_scale, row_ids, live_rows, live_blocks, row_reg.reshape(32, 128))


def solution(mesh):
    return jax.shard_map(
        body,
        mesh=mesh,
        in_specs=(
            P(("row", "col"), None, None, None),
            P(("row", "col"), None),
            P(("row", "col"), None),
            P(("row", "col")),
            P(("row", "col")),
            P(),
        ),
        out_specs=P("row", "col"),
        check_vma=False,
    )
```

time: 101 us -> 75.7 us (0.75)
  Pallas kernels: 94.6 us -> 72.2 us
  local copies, waits for them, and re-layouts: 3.76 us -> 1.87 us
    pallas_call x2 -> x1, Pallas kernels: 94.6 us -> 72.2 us  [body(): pl.pallas_call(kernel, out_shape=jax.ShapeDtypeStruct((512, 256), jnp.flo...]
    unnamed x10 -> x1, local copies, waits for them, and re-layouts: 3.76 us -> 1.87 us
where the time goes in v2:
time: 75.7 us; the launch traced here: 74.7 us
  Pallas kernels  72.2 us (95%)
  local copies, waits for them, and re-layouts  1.87 us (2%)
    pallas_call x1, Pallas kernels, body(): pl.pallas_call(kernel, out_shape=jax.ShapeDtypeStruct((512, 256), jnp.flo...  72.2 us
    unnamed x1, local copies, waits for them, and re-layouts  1.87 us

profile of v2, /device:TPU:0, one launch (start us, length us, event | category | flops | bytes accessed | tf_op | source)
XLA Modules:
  0.0 74.7 jit_solution(679553254992204302)
XLA Ops:
  0.7 72.2 %shard_map.64 = f32[512,256]{1,0:T(8,128)} custom-call(bf16[4,4,128,128]{3,2,1,0:T(8,128)(2,1)} %data_h.1, bf16[4,128]{1,0:T(4,128)(2,1)} %scale_h.1, s32[4,4]{1,0:T(4,128)} %ids_h.1, s32[4]{0:T(128)} %live_rows_h.1, s32[1]{0:T(128)S(6)} %copy.8.live_blocks_h, f32[32,128]{1,0:T(8,128)} %bitcast.1), custom_call_target="tpu_custom_call" | custom-call | tf_op jit(solution)/shard_map/pallas_call | solution.py:399
  72.8 1.9 %copy.9 = f32[512,256]{1,0:T(8,128)} copy(f32[512,256]{1,0:T(8,128)} %shard_map.64) | data formatting | bytes 1048576

commit v3 on v2

v3 whole, which is shorter than its diff:
```python
import jax
import jax.numpy as jnp
from jax import lax
from jax.experimental import pallas as pl
from jax.experimental.pallas import tpu as pltpu
from jax.sharding import PartitionSpec as P

HI = lax.Precision.HIGHEST
NA = 896
ROWS = 528
MESH = pl.DeviceIdType.MESH


def tdot(a, b):
    return lax.dot_general(a, b, (((0,), (0,)), ((), ())), precision=HI,
                           preferred_element_type=jnp.float32)


def fdot(a, b):
    return jnp.dot(a, b, precision=HI, preferred_element_type=jnp.float32)


def lanes(v):
    return jnp.broadcast_to(v, (v.shape[0], 128))


def diag_factor(d, between=None):
    row8 = lax.broadcasted_iota(jnp.int32, (8, 128), 0)
    e = jnp.where(lax.broadcasted_iota(jnp.int32, (128, 128), 0) == lax.broadcasted_iota(jnp.int32, (128, 128), 1), 1.0, 0.0)
    us, es = [], []
    for h in range(4):
        x, y = d[:32], e[:32]
        done_x, done_y = [], []
        for j in range(4):
            lane = 32 * h + 8 * j
            rows = 32 - 8 * j
            row = lax.broadcasted_iota(jnp.int32, (rows, 128), 0)
            cs = [lanes(x[:, lane + i:lane + i + 1]) for i in range(8)]
            scale = jnp.zeros((8, 128), jnp.float32)
            for i in range(8):
                p = cs[i][i:i + 1, :]
                rp = 1.0 / p
                scale = jnp.where(row8 == i, lax.rsqrt(p), scale)
                f = jnp.where(row > i, cs[i] * rp, 0.0)
                for m in range(i + 1, 8):
                    cs[m] = cs[m] - f * cs[m][i:i + 1, :]
                x = x - f * x[i:i + 1, :]
                y = y - f * y[i:i + 1, :]
            done_x.append(x[:8] * scale)
            done_y.append(y[:8] * scale)
            x, y = x[8:], y[8:]
        ux = jnp.concatenate(done_x, axis=0)
        uy = jnp.concatenate(done_y, axis=0)
        us.append(ux)
        es.append(uy)
        if h < 3:
            n = 128 - 32 * (h + 1)
            left = ux[:, :]
            d = d[32:] - tdot(left, ux)[32 * (h + 1):]
            e = e[32:] - tdot(left, uy)[32 * (h + 1):]
    return jnp.concatenate(us, axis=0), jnp.concatenate(es, axis=0)


def kernel(data_h, scale_h, ids_h, live_rows_h, live_blocks_h, reg_h, out,
           data, scale, ids, live_rows, live_blocks, reg, own, panel,
           gat, lbuf, rbuf, part, land0, land1, land, res, x_ref,
           ins, w1s, w1f, w1r, w2s, w2r, ps, pr, own_s, own_r, sib_s, sib_r):
    loads = [pltpu.make_async_copy(a, b, ins.at[i]) for i, (a, b) in enumerate((
        (ids_h, ids), (live_rows_h, live_rows), (live_blocks_h, live_blocks), (scale_h, scale),
        (data_h.at[0], data.at[0]), (data_h.at[1], data.at[1]), (data_h.at[2], data.at[2]),
        (data_h.at[3], data.at[3]), (reg_h, reg)))]
    for load in loads:
        load.start()
    r = lax.axis_index("row")
    q = lax.axis_index("col")
    z, yh = r // 2, lax.rem(r, 2)
    zh, zl = z // 2, lax.rem(z, 2)
    yl, j = q // 8, lax.rem(q, 8)
    x, e = j // 2, lax.rem(j, 2)
    xh, xl = x // 2, lax.rem(x, 2)
    pos = 2 * r + yl
    cls = 2 * yl + xh
    kr, kc = 2 * zl + yh, 2 * xl + e
    sibling = (r, q + 1 - 2 * e)
    order = ((0, 3), (1, 2))

    def ring(d):
        x2 = lax.rem(x + d, 4)
        return (r, yl * 8 + 2 * x2 + e), 2 * x2 + e

    def plane(p):
        return (p // 2, lax.rem(p, 2) * 8 + j)

    def remote(src, dst, send, recv, to):
        return pltpu.make_async_remote_copy(src_ref=src, dst_ref=dst, send_sem=send, recv_sem=recv,
                                            device_id=to, device_id_type=MESH)

    barrier = pltpu.get_barrier_semaphore()
    for d in range(1, 4):
        pl.semaphore_signal(barrier, inc=1, device_id=ring(d)[0], device_id_type=MESH)
    pl.semaphore_signal(barrier, inc=1, device_id=sibling, device_id_type=MESH)
    for d in range(1, 16):
        pl.semaphore_signal(barrier, inc=1, device_id=plane(lax.rem(pos + d, 16)), device_id_type=MESH)

    def prepare(s):
        row = lax.broadcasted_iota(jnp.int32, (16, 128), 0)
        on = s < live_blocks[0]
        meta = jnp.where(row == 0, jnp.broadcast_to(scale[...].astype(jnp.float32)[s:s + 1, :], (16, 128)), 0.0)
        for k in range(4):
            keep = jnp.where(on & (k < live_rows[s]), 1.0, 0.0)
            gat[s, j, k * 128:k * 128 + 128, :] = (data[s, k].astype(jnp.float32) * keep).astype(jnp.bfloat16)
            late = jnp.where(ids[s, k] >= 16, 1.0, 0.0)
            meta = jnp.where(row == k + 1, late, meta)
        gat[s, j, 512:528, :] = meta.astype(jnp.bfloat16)

    def send_w1(s):
        for d in (1, 3, 2, 0):
            remote(gat.at[s, j], gat.at[s, j], w1s.at[s], w1r.at[s, j], sibling if d == 0 else ring(d)[0]).start()

    def w1_arrived(s, j2):
        remote(gat.at[s, j2], gat.at[s, j2], w1f.at[s], w1r.at[s, j2], sibling).wait_recv()

    def forward(s):
        for d in (1, 3, 2):
            j2 = ring(d)[1]
            w1_arrived(s, j2)
            remote(gat.at[s, j2], gat.at[s, j2], w1f.at[s], w1r.at[s, j2], sibling).start()

    def compute(s):
        w1_arrived(s, 2 * x + 1 - e)
        for d in (1, 3, 2):
            w1_arrived(s, 2 * lax.rem(x + d, 4) + 1 - e)

        def build(c, _):
            meta = gat[s, c, 512:528, :].astype(jnp.float32)
            sc = meta[0:1, :]
            at = pl.multiple_of(c * 128, 128)
            for k in range(2):
                t = jnp.where(xh == 0, meta[1 + k:2 + k, :], meta[3 + k:4 + k, :])
                a = gat[s, c, pl.ds(pl.multiple_of((2 * xh + k) * 128, 128), 128), :].astype(jnp.float32)
                g = (a * sc).astype(jnp.bfloat16).astype(jnp.float32)
                lbuf[2 * k * 128:2 * k * 128 + 128, pl.ds(at, 128)] = (g * (1.0 - t)).astype(jnp.bfloat16)
                lbuf[2 * k * 128 + 128:2 * k * 128 + 256, pl.ds(at, 128)] = (g * t).astype(jnp.bfloat16)
            t0 = jnp.where(e == 0, meta[1:2, :], meta[2:3, :])
            t1 = jnp.where(e == 0, meta[3:4, :], meta[4:5, :])
            t = jnp.where(xl == 0, t0, t1)
            a = gat[s, c, pl.ds(pl.multiple_of(kc * 128, 128), 128), :].astype(jnp.float32)
            rbuf[0:128, pl.ds(at, 128)] = (a * (1.0 - t)).astype(jnp.bfloat16)
            rbuf[128:256, pl.ds(at, 128)] = (a * t).astype(jnp.bfloat16)
            return 0

        lax.fori_loop(0, 8, build, 0)
        for k in range(2):
            for t in range(2):
                row = (2 * k + t) * 128
                acc = lax.dot_general(lbuf[row:row + 128, :], rbuf[...], (((1,), (1,)), ((), ())),
                                      preferred_element_type=jnp.float32)
                for u in range(2):
                    part[s, :, order[t][u], k] = acc[:, u * 128:u * 128 + 128].reshape(16, 8, 128)

    def w2(s, d, first, count, to_buf, sem):
        to = lax.rem(pos + d, 16)
        return remote(part.at[s, to, first:first + count], to_buf.at[pos], w2s.at[sem], w2r.at[sem], plane(to))

    def w2_wait(buf, sem):
        remote(buf.at[0:15], buf.at[0:15], w2s.at[sem], w2r.at[sem], sibling).wait_recv()

    def w2_sum(mine, buf):
        total = mine
        for d in range(1, 16):
            total = total + buf[lax.rem(pos + d, 16)]
        return total

    def owner_of(s, k):
        sh, sl = s // 2, lax.rem(s, 2)
        to = ((2 * sl + xh) * 2 + k, sh * 8 + (2 * sl + xl) * 2 + e)
        return to, (to[0] != r) | (to[1] != q)

    def to_panel(t):
        for d in range(8):
            to = ((d // 4) * 2 + (d // 2) % 2, (d % 2) * 2 + 1 - e)
            remote(res.at[0, t], panel.at[e, t, xl, xh, pos], ps.at[t], pr.at[t], to).start()

    def panel_sent(t):
        remote(land0.at[0:8], land0.at[0:8], ps.at[t], pr.at[t], sibling).wait_send()

    def leading():
        for d in range(1, 16):
            w2(0, d, 0, 1, land0, 0).start()
        w2_wait(land0, 0)
        res[0, 0:1] = w2_sum(part[0, pos, 0:1], land0)
        to_panel(0)

    def below_start():
        panel_sent(0)
        for d in range(1, 16):
            w2(0, d, 1, 2, land1, 1).start()

    def below():
        w2_wait(land1, 1)
        res[0, 1:3] = w2_sum(part[0, pos, 1:3], land1)
        to_panel(1)
        for k in range(2):
            to, away = owner_of(0, k)
            pl.when(away)(remote(res.at[0, 2, k], own.at[pos, 2], own_s.at[0, k], own_r, to).start)

            @pl.when(jnp.logical_not(away))
            def _():
                own[pos, 2] = res[0, 2, k]

    def send_w2(s):
        for d in range(1, 16):
            w2(s, d, 0, 4, land.at[s - 1], s + 1).start()

    def others(s, _):
        w2_wait(land.at[s - 1], s + 1)
        res[s] = w2_sum(part[s, pos], land.at[s - 1])
        for k in range(2):
            to, away = owner_of(s, k)
            pl.when(away)(remote(res.at[s, :, k], own.at[pos], own_s.at[s, k], own_r, to).start)

            @pl.when(jnp.logical_not(away))
            def _():
                own[pos] = res[s, :, k]
        return 0

    def sent():
        def one(s, _):
            remote(gat.at[s, 0:4], gat.at[s, 0:4], w1s.at[s], w1r.at[s, 0], sibling).wait_send()
            remote(gat.at[s, 0:3], gat.at[s, 0:3], w1f.at[s], w1r.at[s, 0], sibling).wait_send()
            return 0

        lax.fori_loop(0, 4, one, 0)
        for buf, sem in ((land0, 0), (land1, 1), (land.at[0], 2), (land.at[1], 3), (land.at[2], 4)):
            remote(buf.at[0:15], buf.at[0:15], w2s.at[sem], w2r.at[sem], sibling).wait_send()
        def pieces(s, _):
            for k in range(2):
                to, away = owner_of(s, k)
                pl.when(away)(remote(res.at[s, :, k], own.at[pos], own_s.at[s, k], own_r, to).wait_send)
            return 0

        for k in range(2):
            to, away = owner_of(0, k)
            pl.when(away)(remote(res.at[0, 2, k], own.at[pos, 2], own_s.at[0, k], own_r, to).wait_send)
        lax.fori_loop(1, 4, pieces, 0)

    eye = (lax.broadcasted_iota(jnp.int32, (128, 128), 0) == lax.broadcasted_iota(jnp.int32, (128, 128), 1))

    def diag(block):
        return jnp.where(eye, jnp.broadcast_to(reg[pl.ds(block, 1), :], (128, 128)), 0.0)

    def blk(t, a, b):
        return panel[b % 2 if isinstance(b, int) else lax.rem(b, 2), t, b // 2, a // 2, :,
                     a % 2 if isinstance(a, int) else lax.rem(a, 2)].reshape(128, 128)

    def mine(t, u):
        base = own[:, order[t][u]].reshape(128, 128)
        if t == u:
            base = base + jnp.where(kr == kc, 1.0, 0.0) * diag(cls * 4 + kr + 16 * t)
        return base

    def panel_half(t):
        remote(panel.at[1 - e, t], panel.at[1 - e, t], ps.at[t], pr.at[t], sibling).wait_recv()
        remote(panel.at[1 - e, t], panel.at[1 - e, t], sib_s.at[t], sib_r.at[t], sibling).start()

    def panel_rest(t):
        copy = remote(panel.at[1 - e, t], panel.at[e, t], sib_s.at[t], sib_r.at[t], sibling)
        copy.wait_recv()
        copy.wait_send()

    def own_wait(view):
        alone = xh == zl

        @pl.when(alone)
        def _():
            ref = view(15)
            remote(ref, ref, own_s.at[0, 0], own_r, sibling).wait_recv()

        @pl.when(jnp.logical_not(alone))
        def _():
            ref = view(16)
            remote(ref, ref, own_s.at[0, 0], own_r, sibling).wait_recv()

    def factor():
        panel_half(0)
        forward(1)
        below()
        panel_rest(0)
        for i in range(4):
            for k in range(i, 4):
                s = 0.5 * (blk(0, i, k) + blk(0, k, i).T)
                if i == k:
                    s = s + diag(i)
                x_ref[i * 128:i * 128 + 128, k * 128:k * 128 + 128] = s
            x_ref[i * 128:i * 128 + 128, 512:640] = blk(0, kr, i).T + jnp.where(kr == i, 1.0, 0.0) * diag(i)
        inverses = []
        for n in range(4):
            lo, hi = n * 128, n * 128 + 128
            width = 640 if n < 2 else NA
            ud, li = diag_factor(x_ref[lo:hi, lo:hi])
            inverses.append(li)
            if n == 2:
                panel_rest(1)
                for k in range(4):
                    x_ref[k * 128:k * 128 + 128, 640:768] = blk(1, kr, k).T
                    x_ref[k * 128:k * 128 + 128, 768:896] = blk(1, kc, k).T
                for k in range(2):
                    rows, later = slice(k * 128, k * 128 + 128), slice(k * 128 + 128, 512)
                    u = fdot(inverses[k], x_ref[rows, 640:NA])
                    x_ref[rows, 640:NA] = u
                    x_ref[later, 640:NA] = x_ref[later, 640:NA] - tdot(x_ref[rows, later], u)
            u = fdot(li, x_ref[lo:hi, hi:width])
            x_ref[lo:hi, hi:width] = u
            for nxt in range(n + 1, 4):
                c = nxt * 128
                x_ref[c:c + 128, c:width] = x_ref[c:c + 128, c:width] - tdot(u[:, c - hi:c - hi + 128], u[:, c - hi:])
            if n == 0:
                panel_sent(1)
                compute(1)
                send_w2(1)
                forward(2)
                compute(2)
                send_w2(2)
                forward(3)
            if n == 1:
                panel_half(1)
                compute(3)
                send_w2(3)
            if n == 2:
                others(1, 0)
                others(2, 0)
            if n == 3:
                others(3, 0)
        at = pl.multiple_of(kc * 128, 128)
        out[0:128, 0:128] = x_ref[pl.ds(at, 128), 512:640].T
        out[256:384, 0:128] = x_ref[pl.ds(at, 128), 640:768].T
        left = tdot(x_ref[:, 640:768], x_ref[:, 768:896])
        own_wait(lambda n: own.at[0:n, 2])
        out[256:384, 128:256] = mine(1, 1) - left

    for i in range(5):
        loads[i].wait()
    prepare(0)
    pl.semaphore_wait(barrier, 19)
    send_w1(0)
    for s in range(1, 4):
        loads[s + 4].wait()
        prepare(s)
    loads[8].wait()
    out[...] = jnp.zeros_like(out)
    forward(0)
    send_w1(1)
    compute(0)
    leading()
    below_start()
    send_w1(2)
    send_w1(3)

    first_owner = (cls == 0) & (zh == 0)
    pl.when(first_owner)(factor)

    @pl.when(jnp.logical_not(first_owner))
    def _():
        forward(1)
        compute(1)
        below()
        panel_sent(1)
        send_w2(1)
        forward(2)
        compute(2)
        send_w2(2)
        forward(3)
        compute(3)
        send_w2(3)
        lax.fori_loop(1, 4, others, 0)

    @pl.when((cls > 0) & (zh == xh))
    def _():
        own_wait(lambda n: own.at[0:n])
        for t in range(2):
            at = pl.multiple_of((cls // 2 + 2 * t) * 128, 128)
            for u in range(2):
                out[pl.ds(at, 128), u * 128:u * 128 + 128] = mine(t, u)

    sent()


def body(col_data, col_scale, row_ids, live_rows, live_blocks, row_reg):
    anywhere = pl.BlockSpec(memory_space=pl.ANY)
    dma = pltpu.SemaphoreType.DMA
    return pl.pallas_call(
        kernel,
        out_shape=jax.ShapeDtypeStruct((512, 256), jnp.float32),
        in_specs=[anywhere] * 6,
        out_specs=pl.BlockSpec(memory_space=pltpu.VMEM),
        scratch_shapes=[
            pltpu.VMEM((4, 4, 128, 128), jnp.bfloat16),
            pltpu.VMEM((4, 128), jnp.bfloat16),
            pltpu.SMEM((4, 4), jnp.int32),
            pltpu.SMEM((4,), jnp.int32),
            pltpu.SMEM((1,), jnp.int32),
            pltpu.VMEM((32, 128), jnp.float32),
            pltpu.VMEM((16, 4, 8, 128), jnp.float32),
            pltpu.VMEM((2, 2, 2, 2, 16, 2, 8, 128), jnp.float32),
            pltpu.VMEM((4, 8, ROWS, 128), jnp.bfloat16),
            pltpu.VMEM((512, 1024), jnp.bfloat16),
            pltpu.VMEM((256, 1024), jnp.bfloat16),
            pltpu.VMEM((4, 16, 4, 2, 8, 128), jnp.float32),
            pltpu.VMEM((16, 1, 2, 8, 128), jnp.float32),
            pltpu.VMEM((16, 2, 2, 8, 128), jnp.float32),
            pltpu.VMEM((3, 16, 4, 2, 8, 128), jnp.float32),
            pltpu.VMEM((4, 4, 2, 8, 128), jnp.float32),
            pltpu.VMEM((512, NA), jnp.float32),
            dma((9,)),
            dma((4,)), dma((4,)), dma((4, 8)), dma((5,)), dma((5,)), dma((2,)), dma((2,)),
            dma((4, 2)), dma, dma((2,)), dma((2,)),
        ],
        compiler_params=pltpu.CompilerParams(
            collective_id=0, has_side_effects=True, vmem_limit_bytes=60 * 1024 * 1024),
    )(col_data, col_scale, row_ids, live_rows, live_blocks, row_reg.reshape(32, 128))


def solution(mesh):
    return jax.shard_map(
        body,
        mesh=mesh,
        in_specs=(
            P(("row", "col"), None, None, None),
            P(("row", "col"), None),
            P(("row", "col"), None),
            P(("row", "col")),
            P(("row", "col")),
            P(),
        ),
        out_specs=P("row", "col"),
        check_vma=False,
    )
```

time: 75.7 us -> 68.3 us (0.902); the launches traced: 74.7 us -> 68.1 us
  Pallas kernels: 72.2 us -> 65.6 us
    pallas_call x1, Pallas kernels: 72.2 us -> 65.6 us  [body(): pl.pallas_call(kernel, out_shape=jax.ShapeDtypeStruct((512, 256), jnp.flo...]
where the time goes in v3:
time: 68.3 us; the launch traced here: 68.1 us
  Pallas kernels  65.6 us (96%)
  local copies, waits for them, and re-layouts  1.87 us (3%)
    pallas_call x1, Pallas kernels, body(): pl.pallas_call(kernel, out_shape=jax.ShapeDtypeStruct((512, 256), jnp.flo...  65.6 us
    unnamed x1, local copies, waits for them, and re-layouts  1.87 us

profile of v3, /device:TPU:0, one launch (start us, length us, event | category | flops | bytes accessed | tf_op | source)
XLA Modules:
  0.0 68.1 jit_solution(3281523395796659230)
XLA Ops:
  0.7 65.6 %shard_map.64 = f32[512,256]{1,0:T(8,128)} custom-call(bf16[4,4,128,128]{3,2,1,0:T(8,128)(2,1)} %data_h.1, bf16[4,128]{1,0:T(4,128)(2,1)} %scale_h.1, s32[4,4]{1,0:T(4,128)} %ids_h.1, s32[4]{0:T(128)} %live_rows_h.1, s32[1]{0:T(128)S(6)} %copy.8.live_blocks_h, f32[32,128]{1,0:T(8,128)} %bitcast.1), custom_call_target="tpu_custom_call" | custom-call | tf_op jit(solution)/shard_map/pallas_call | solution.py:391
  66.3 1.9 %copy.9 = f32[512,256]{1,0:T(8,128)} copy(f32[512,256]{1,0:T(8,128)} %shard_map.64) | data formatting | bytes 1048576

commit v4 on v3

--- a/solution.py
+++ b/solution.py
@@ -75,34 +75,44 @@
     q = lax.axis_index("col")
     z, yh = r // 2, lax.rem(r, 2)
     zh, zl = z // 2, lax.rem(z, 2)
-    yl, j = q // 8, lax.rem(q, 8)
-    x, e = j // 2, lax.rem(j, 2)
+    yl = q // 8
+    x, e = lax.rem(q, 8) // 2, lax.rem(q, 2)
     xh, xl = x // 2, lax.rem(x, 2)
-    pos = 2 * r + yl
+    y = 2 * yh + yl
     cls = 2 * yl + xh
     kr, kc = 2 * zl + yh, 2 * xl + e
     sibling = (r, q + 1 - 2 * e)
     order = ((0, 3), (1, 2))
-
-    def ring(d):
-        x2 = lax.rem(x + d, 4)
-        return (r, yl * 8 + 2 * x2 + e), 2 * x2 + e
-
-    def plane(p):
-        return (p // 2, lax.rem(p, 2) * 8 + j)
+    along = (x, y, z, z)
+    place = (4 * z + y, 4 * z + x, 4 * y + x, 4 * y + x)
+
+    def device(xx, yy, zz):
+        return (2 * zz + yy // 2, lax.rem(yy, 2) * 8 + 2 * xx + e)
+
+    def ring(s, d):
+        u = lax.rem(along[s] + d, 4)
+        to = (device(u, y, z), device(x, u, z), device(x, y, u), device(x, y, u))[s]
+        return to, 2 * u + e
+
+    def plane(s, p):
+        a, b = p // 4, lax.rem(p, 4)
+        return (device(x, b, a), device(b, y, a), device(b, a, z), device(b, a, z))[s]
 
     def remote(src, dst, send, recv, to):
         return pltpu.make_async_remote_copy(src_ref=src, dst_ref=dst, send_sem=send, recv_sem=recv,
                                             device_id=to, device_id_type=MESH)
 
     barrier = pltpu.get_barrier_semaphore()
-    for d in range(1, 4):
-        pl.semaphore_signal(barrier, inc=1, device_id=ring(d)[0], device_id_type=MESH)
     pl.semaphore_signal(barrier, inc=1, device_id=sibling, device_id_type=MESH)
-    for d in range(1, 16):
-        pl.semaphore_signal(barrier, inc=1, device_id=plane(lax.rem(pos + d, 16)), device_id_type=MESH)
+    for dx in range(4):
+        for dy in range(4):
+            for dz in range(4):
+                if 0 < (dx > 0) + (dy > 0) + (dz > 0) < 3:
+                    to = device(lax.rem(x + dx, 4), lax.rem(y + dy, 4), lax.rem(z + dz, 4))
+                    pl.semaphore_signal(barrier, inc=1, device_id=to, device_id_type=MESH)
 
     def prepare(s):
+        j = 2 * along[s] + e
         row = lax.broadcasted_iota(jnp.int32, (16, 128), 0)
         on = s < live_blocks[0]
         meta = jnp.where(row == 0, jnp.broadcast_to(scale[...].astype(jnp.float32)[s:s + 1, :], (16, 128)), 0.0)
@@ -114,37 +124,39 @@
         gat[s, j, 512:528, :] = meta.astype(jnp.bfloat16)
 
     def send_w1(s):
+        j = 2 * along[s] + e
         for d in (1, 3, 2, 0):
-            remote(gat.at[s, j], gat.at[s, j], w1s.at[s], w1r.at[s, j], sibling if d == 0 else ring(d)[0]).start()
+            remote(gat.at[s, j], gat.at[s, j], w1s.at[s], w1r.at[s, j], sibling if d == 0 else ring(s, d)[0]).start()
 
     def w1_arrived(s, j2):
         remote(gat.at[s, j2], gat.at[s, j2], w1f.at[s], w1r.at[s, j2], sibling).wait_recv()
 
     def forward(s):
         for d in (1, 3, 2):
-            j2 = ring(d)[1]
+            j2 = ring(s, d)[1]
             w1_arrived(s, j2)
             remote(gat.at[s, j2], gat.at[s, j2], w1f.at[s], w1r.at[s, j2], sibling).start()
 
     def compute(s):
-        w1_arrived(s, 2 * x + 1 - e)
-        for d in (1, 3, 2):
-            w1_arrived(s, 2 * lax.rem(x + d, 4) + 1 - e)
+        u = along[s]
+        uh, ul = u // 2, lax.rem(u, 2)
+        for d in (0, 1, 3, 2):
+            w1_arrived(s, 2 * lax.rem(u + d, 4) + 1 - e)
 
         def build(c, _):
             meta = gat[s, c, 512:528, :].astype(jnp.float32)
             sc = meta[0:1, :]
             at = pl.multiple_of(c * 128, 128)
             for k in range(2):
-                t = jnp.where(xh == 0, meta[1 + k:2 + k, :], meta[3 + k:4 + k, :])
-                a = gat[s, c, pl.ds(pl.multiple_of((2 * xh + k) * 128, 128), 128), :].astype(jnp.float32)
+                t = jnp.where(uh == 0, meta[1 + k:2 + k, :], meta[3 + k:4 + k, :])
+                a = gat[s, c, pl.ds(pl.multiple_of((2 * uh + k) * 128, 128), 128), :].astype(jnp.float32)
                 g = (a * sc).astype(jnp.bfloat16).astype(jnp.float32)
                 lbuf[2 * k * 128:2 * k * 128 + 128, pl.ds(at, 128)] = (g * (1.0 - t)).astype(jnp.bfloat16)
                 lbuf[2 * k * 128 + 128:2 * k * 128 + 256, pl.ds(at, 128)] = (g * t).astype(jnp.bfloat16)
             t0 = jnp.where(e == 0, meta[1:2, :], meta[2:3, :])
             t1 = jnp.where(e == 0, meta[3:4, :], meta[4:5, :])
-            t = jnp.where(xl == 0, t0, t1)
-            a = gat[s, c, pl.ds(pl.multiple_of(kc * 128, 128), 128), :].astype(jnp.float32)
+            t = jnp.where(ul == 0, t0, t1)
+            a = gat[s, c, pl.ds(pl.multiple_of((2 * ul + e) * 128, 128), 128), :].astype(jnp.float32)
             rbuf[0:128, pl.ds(at, 128)] = (a * (1.0 - t)).astype(jnp.bfloat16)
             rbuf[128:256, pl.ds(at, 128)] = (a * t).astype(jnp.bfloat16)
             return 0
@@ -159,70 +171,70 @@
                     part[s, :, order[t][u], k] = acc[:, u * 128:u * 128 + 128].reshape(16, 8, 128)
 
     def w2(s, d, first, count, to_buf, sem):
-        to = lax.rem(pos + d, 16)
-        return remote(part.at[s, to, first:first + count], to_buf.at[pos], w2s.at[sem], w2r.at[sem], plane(to))
+        to = lax.rem(place[s] + d, 16)
+        return remote(part.at[s, to, first:first + count], to_buf.at[place[s]], w2s.at[sem], w2r.at[sem], plane(s, to))
 
     def w2_wait(buf, sem):
         remote(buf.at[0:15], buf.at[0:15], w2s.at[sem], w2r.at[sem], sibling).wait_recv()
 
-    def w2_sum(mine, buf):
+    def w2_sum(s, mine, buf):
         total = mine
         for d in range(1, 16):
-            total = total + buf[lax.rem(pos + d, 16)]
+            total = total + buf[lax.rem(place[s] + d, 16)]
         return total
 
     def owner_of(s, k):
-        sh, sl = s // 2, lax.rem(s, 2)
-        to = ((2 * sl + xh) * 2 + k, sh * 8 + (2 * sl + xl) * 2 + e)
+        uh, ul = along[s] // 2, lax.rem(along[s], 2)
+        to = device(2 * (s % 2) + ul, 2 * k + s // 2, 2 * (s % 2) + uh)
         return to, (to[0] != r) | (to[1] != q)
 
     def to_panel(t):
         for d in range(8):
             to = ((d // 4) * 2 + (d // 2) % 2, (d % 2) * 2 + 1 - e)
-            remote(res.at[0, t], panel.at[e, t, xl, xh, pos], ps.at[t], pr.at[t], to).start()
+            remote(res.at[0, t], panel.at[e, t, xl, xh, place[0]], ps.at[t], pr.at[t], to).start()
 
     def panel_sent(t):
         remote(land0.at[0:8], land0.at[0:8], ps.at[t], pr.at[t], sibling).wait_send()
 
-    def leading():
+    def leading_start():
         for d in range(1, 16):
             w2(0, d, 0, 1, land0, 0).start()
+
+    def leading():
         w2_wait(land0, 0)
-        res[0, 0:1] = w2_sum(part[0, pos, 0:1], land0)
+        res[0, 0:1] = w2_sum(0, part[0, place[0], 0:1], land0)
         to_panel(0)
 
     def below_start():
-        panel_sent(0)
         for d in range(1, 16):
             w2(0, d, 1, 2, land1, 1).start()
 
     def below():
         w2_wait(land1, 1)
-        res[0, 1:3] = w2_sum(part[0, pos, 1:3], land1)
+        res[0, 1:3] = w2_sum(0, part[0, place[0], 1:3], land1)
         to_panel(1)
         for k in range(2):
             to, away = owner_of(0, k)
-            pl.when(away)(remote(res.at[0, 2, k], own.at[pos, 2], own_s.at[0, k], own_r, to).start)
+            pl.when(away)(remote(res.at[0, 2, k], own.at[place[0], 2], own_s.at[0, k], own_r, to).start)
 
             @pl.when(jnp.logical_not(away))
             def _():
-                own[pos, 2] = res[0, 2, k]
+                own[place[0], 2] = res[0, 2, k]
 
     def send_w2(s):
         for d in range(1, 16):
             w2(s, d, 0, 4, land.at[s - 1], s + 1).start()
 
-    def others(s, _):
+    def others(s):
         w2_wait(land.at[s - 1], s + 1)
-        res[s] = w2_sum(part[s, pos], land.at[s - 1])
+        res[s] = w2_sum(s, part[s, place[s]], land.at[s - 1])
         for k in range(2):
             to, away = owner_of(s, k)
-            pl.when(away)(remote(res.at[s, :, k], own.at[pos], own_s.at[s, k], own_r, to).start)
+            pl.when(away)(remote(res.at[s, :, k], own.at[place[s]], own_s.at[s, k], own_r, to).start)
 
             @pl.when(jnp.logical_not(away))
             def _():
-                own[pos] = res[s, :, k]
-        return 0
+                own[place[s]] = res[s, :, k]
 
     def sent():
         def one(s, _):
@@ -233,16 +245,13 @@
         lax.fori_loop(0, 4, one, 0)
         for buf, sem in ((land0, 0), (land1, 1), (land.at[0], 2), (land.at[1], 3), (land.at[2], 4)):
             remote(buf.at[0:15], buf.at[0:15], w2s.at[sem], w2r.at[sem], sibling).wait_send()
-        def pieces(s, _):
+        for k in range(2):
+            to, away = owner_of(0, k)
+            pl.when(away)(remote(res.at[0, 2, k], own.at[place[0], 2], own_s.at[0, k], own_r, to).wait_send)
+        for s in range(1, 4):
             for k in range(2):
                 to, away = owner_of(s, k)
-                pl.when(away)(remote(res.at[s, :, k], own.at[pos], own_s.at[s, k], own_r, to).wait_send)
-            return 0
-
-        for k in range(2):
-            to, away = owner_of(0, k)
-            pl.when(away)(remote(res.at[0, 2, k], own.at[pos, 2], own_s.at[0, k], own_r, to).wait_send)
-        lax.fori_loop(1, 4, pieces, 0)
+                pl.when(away)(remote(res.at[s, :, k], own.at[place[s]], own_s.at[s, k], own_r, to).wait_send)
 
     eye = (lax.broadcasted_iota(jnp.int32, (128, 128), 0) == lax.broadcasted_iota(jnp.int32, (128, 128), 1))
 
@@ -269,7 +278,8 @@
         copy.wait_send()
 
     def own_wait(view):
-        alone = xh == zl
+        mark = 2 * zl + xl
+        alone = ((cls == 0) & (x == mark)) | ((cls == 1) & (y == mark)) | ((cls > 1) & (z == mark))
 
         @pl.when(alone)
         def _():
@@ -283,7 +293,7 @@
 
     def factor():
         panel_half(0)
-        forward(1)
+        compute(1)
         below()
         panel_rest(0)
         for i in range(4):
@@ -316,21 +326,17 @@
                 x_ref[c:c + 128, c:width] = x_ref[c:c + 128, c:width] - tdot(u[:, c - hi:c - hi + 128], u[:, c - hi:])
             if n == 0:
                 panel_sent(1)
-                compute(1)
                 send_w2(1)
-                forward(2)
-                compute(2)
-                send_w2(2)
-                forward(3)
+                compute(3)
+                send_w2(3)
             if n == 1:
                 panel_half(1)
-                compute(3)
-                send_w2(3)
+                others(2)
             if n == 2:
-                others(1, 0)
-                others(2, 0)
+                others(1)
+                others(3)
             if n == 3:
-                others(3, 0)
+                pass
         at = pl.multiple_of(kc * 128, 128)
         out[0:128, 0:128] = x_ref[pl.ds(at, 128), 512:640].T
         out[256:384, 0:128] = x_ref[pl.ds(at, 128), 640:768].T
@@ -341,38 +347,42 @@
     for i in range(5):
         loads[i].wait()
     prepare(0)
-    pl.semaphore_wait(barrier, 19)
+    pl.semaphore_wait(barrier, 37)
     send_w1(0)
     for s in range(1, 4):
         loads[s + 4].wait()
         prepare(s)
+        if s in (1, 2):
+            send_w1(s)
     loads[8].wait()
     out[...] = jnp.zeros_like(out)
     forward(0)
-    send_w1(1)
+    send_w1(3)
     compute(0)
+    leading_start()
     leading()
+    forward(1)
+    forward(2)
+    panel_sent(0)
     below_start()
-    send_w1(2)
-    send_w1(3)
+    compute(2)
+    send_w2(2)
+    forward(3)
 
     first_owner = (cls == 0) & (zh == 0)
     pl.when(first_owner)(factor)
 
     @pl.when(jnp.logical_not(first_owner))
     def _():
-        forward(1)
         compute(1)
         below()
         panel_sent(1)
         send_w2(1)
-        forward(2)
-        compute(2)
-        send_w2(2)
-        forward(3)
         compute(3)
         send_w2(3)
-        lax.fori_loop(1, 4, others, 0)
+        others(2)
+        others(1)
+        others(3)
 
     @pl.when((cls > 0) & (zh == xh))
     def _():
@@ -386,7 +396,7 @@
 
 
 def body(col_data, col_scale, row_ids, live_rows, live_blocks, row_reg):
-    anywhere = pl.BlockSpec(memory_space=pl.ANY)
+    anywhere = pl.BlockSpec(memory_space=pltpu.HBM)
     dma = pltpu.SemaphoreType.DMA
     return pl.pallas_call(
         kernel,

time: 68.3 us -> 66.4 us (0.972); the launches traced: 68.1 us -> 65.5 us
  Pallas kernels: 65.6 us -> 63 us
    pallas_call x1, Pallas kernels: 65.6 us -> 63 us  [body(): pl.pallas_call(kernel, out_shape=jax.ShapeDtypeStruct((512, 256), jnp.flo...]
where the time goes in v4:
time: 66.4 us; the launch traced here: 65.5 us
  Pallas kernels  63 us (95%)
  local copies, waits for them, and re-layouts  1.87 us (3%)
    pallas_call x1, Pallas kernels, body(): pl.pallas_call(kernel, out_shape=jax.ShapeDtypeStruct((512, 256), jnp.flo...  63 us
    unnamed x1, local copies, waits for them, and re-layouts  1.87 us

profile of v4, /device:TPU:0, one launch (start us, length us, event | category | flops | bytes accessed | tf_op | source)
XLA Modules:
  0.0 65.5 jit_solution(833499100037347440)
XLA Ops:
  0.7 63.0 %shard_map.64 = f32[512,256]{1,0:T(8,128)} custom-call(bf16[4,4,128,128]{3,2,1,0:T(8,128)(2,1)} %data_h.1, bf16[4,128]{1,0:T(4,128)(2,1)} %scale_h.1, s32[4,4]{1,0:T(4,128)} %ids_h.1, s32[4]{0:T(128)} %live_rows_h.1, s32[1]{0:T(128)S(6)} %copy.8.live_blocks_h, f32[32,128]{1,0:T(8,128)} %bitcast.1), custom_call_target="tpu_custom_call" | custom-call | tf_op jit(solution)/shard_map/pallas_call | solution.py:401
  63.6 1.9 %copy.9 = f32[512,256]{1,0:T(8,128)} copy(f32[512,256]{1,0:T(8,128)} %shard_map.64) | data formatting | bytes 1048576

commit v5 on v4

--- a/solution.py
+++ b/solution.py
@@ -24,7 +24,7 @@
     return jnp.broadcast_to(v, (v.shape[0], 128))
 
 
-def diag_factor(d, between=None):
+def diag_factor(d):
     row8 = lax.broadcasted_iota(jnp.int32, (8, 128), 0)
     e = jnp.where(lax.broadcasted_iota(jnp.int32, (128, 128), 0) == lax.broadcasted_iota(jnp.int32, (128, 128), 1), 1.0, 0.0)
     us, es = [], []
@@ -37,15 +37,22 @@
             row = lax.broadcasted_iota(jnp.int32, (rows, 128), 0)
             cs = [lanes(x[:, lane + i:lane + i + 1]) for i in range(8)]
             scale = jnp.zeros((8, 128), jnp.float32)
-            for i in range(8):
-                p = cs[i][i:i + 1, :]
-                rp = 1.0 / p
-                scale = jnp.where(row8 == i, lax.rsqrt(p), scale)
-                f = jnp.where(row > i, cs[i] * rp, 0.0)
-                for m in range(i + 1, 8):
-                    cs[m] = cs[m] - f * cs[m][i:i + 1, :]
-                x = x - f * x[i:i + 1, :]
-                y = y - f * y[i:i + 1, :]
+            for i in range(0, 8, 2):
+                a, b, c = cs[i][i:i + 1, :], cs[i + 1][i:i + 1, :], cs[i + 1][i + 1:i + 2, :]
+                det = a * c - b * b
+                ra, rdet = 1.0 / a, 1.0 / det
+                w = b * ra
+                scale = jnp.where(row8 == i, lax.rsqrt(a), scale)
+                scale = jnp.where(row8 == i + 1, lax.rsqrt(det * ra), scale)
+                f = jnp.where(row > i, cs[i] * ra, 0.0)
+                g = jnp.where(row > i + 1, (cs[i + 1] - cs[i] * w) * (a * rdet), 0.0)
+                for m in range(i + 2, 8):
+                    t = cs[m][i:i + 1, :]
+                    cs[m] = cs[m] - f * t - g * (cs[m][i + 1:i + 2, :] - w * t)
+                t = x[i:i + 1, :]
+                x = x - f * t - g * (x[i + 1:i + 2, :] - w * t)
+                t = y[i:i + 1, :]
+                y = y - f * t - g * (y[i + 1:i + 2, :] - w * t)
             done_x.append(x[:8] * scale)
             done_y.append(y[:8] * scale)
             x, y = x[8:], y[8:]
@@ -54,10 +61,8 @@
         us.append(ux)
         es.append(uy)
         if h < 3:
-            n = 128 - 32 * (h + 1)
-            left = ux[:, :]
-            d = d[32:] - tdot(left, ux)[32 * (h + 1):]
-            e = e[32:] - tdot(left, uy)[32 * (h + 1):]
+            d = d[32:] - tdot(ux, ux)[32 * (h + 1):]
+            e = e[32:] - tdot(ux, uy)[32 * (h + 1):]
     return jnp.concatenate(us, axis=0), jnp.concatenate(es, axis=0)
 
 
@@ -162,13 +167,17 @@
             return 0
 
         lax.fori_loop(0, 8, build, 0)
+        multiply(s, 0)
+        if s > 0:
+            multiply(s, 1)
+
+    def multiply(s, t):
         for k in range(2):
-            for t in range(2):
-                row = (2 * k + t) * 128
-                acc = lax.dot_general(lbuf[row:row + 128, :], rbuf[...], (((1,), (1,)), ((), ())),
-                                      preferred_element_type=jnp.float32)
-                for u in range(2):
-                    part[s, :, order[t][u], k] = acc[:, u * 128:u * 128 + 128].reshape(16, 8, 128)
+            row = (2 * k + t) * 128
+            acc = lax.dot_general(lbuf[row:row + 128, :], rbuf[...], (((1,), (1,)), ((), ())),
+                                  preferred_element_type=jnp.float32)
+            for u in range(2):
+                part[s, :, order[t][u], k] = acc[:, u * 128:u * 128 + 128].reshape(16, 8, 128)
 
     def w2(s, d, first, count, to_buf, sem):
         to = lax.rem(place[s] + d, 16)
@@ -360,6 +369,7 @@
     send_w1(3)
     compute(0)
     leading_start()
+    multiply(0, 1)
     leading()
     forward(1)
     forward(2)

time: 66.4 us -> 64 us (0.964); the launches traced: 65.5 us -> 63.8 us
  Pallas kernels: 63 us -> 61.3 us
    pallas_call x1, Pallas kernels: 63 us -> 61.3 us  [body(): pl.pallas_call(kernel, out_shape=jax.ShapeDtypeStruct((512, 256), jnp.flo...]
where the time goes in v5:
time: 64 us; the launch traced here: 63.8 us
  Pallas kernels  61.3 us (96%)
  local copies, waits for them, and re-layouts  1.87 us (3%)
  between operations  0.66 us (1%)
    pallas_call x1, Pallas kernels, body(): pl.pallas_call(kernel, out_shape=jax.ShapeDtypeStruct((512, 256), jnp.flo...  61.3 us
    unnamed x1, local copies, waits for them, and re-layouts  1.87 us

profile of v5, /device:TPU:0, one launch (start us, length us, event | category | flops | bytes accessed | tf_op | source)
XLA Modules:
  0.0 63.8 jit_solution(2550301435013633477)
XLA Ops:
  0.7 61.3 %shard_map.64 = f32[512,256]{1,0:T(8,128)} custom-call(bf16[4,4,128,128]{3,2,1,0:T(8,128)(2,1)} %data_h.1, bf16[4,128]{1,0:T(4,128)(2,1)} %scale_h.1, s32[4,4]{1,0:T(4,128)} %ids_h.1, s32[4]{0:T(128)} %live_rows_h.1, s32[1]{0:T(128)S(6)} %copy.8.live_blocks_h, f32[32,128]{1,0:T(8,128)} %bitcast.1), custom_call_target="tpu_custom_call" | custom-call | tf_op jit(solution)/shard_map/pallas_call | solution.py:411
  62.0 1.9 %copy.9 = f32[512,256]{1,0:T(8,128)} copy(f32[512,256]{1,0:T(8,128)} %shard_map.64) | data formatting | bytes 1048576

commit v6 on v5

--- a/solution.py
+++ b/solution.py
@@ -61,8 +61,9 @@
         us.append(ux)
         es.append(uy)
         if h < 3:
-            d = d[32:] - tdot(ux, ux)[32 * (h + 1):]
-            e = e[32:] - tdot(ux, uy)[32 * (h + 1):]
+            both = fdot(ux.T[32 * (h + 1):], jnp.concatenate([ux, uy], axis=1))
+            d = d[32:] - both[:, :128]
+            e = e[32:] - both[:, 128:]
     return jnp.concatenate(us, axis=0), jnp.concatenate(es, axis=0)
 
 
@@ -74,8 +75,6 @@
         (ids_h, ids), (live_rows_h, live_rows), (live_blocks_h, live_blocks), (scale_h, scale),
         (data_h.at[0], data.at[0]), (data_h.at[1], data.at[1]), (data_h.at[2], data.at[2]),
         (data_h.at[3], data.at[3]), (reg_h, reg)))]
-    for load in loads:
-        load.start()
     r = lax.axis_index("row")
     q = lax.axis_index("col")
     z, yh = r // 2, lax.rem(r, 2)
@@ -88,6 +87,7 @@
     kr, kc = 2 * zl + yh, 2 * xl + e
     sibling = (r, q + 1 - 2 * e)
     order = ((0, 3), (1, 2))
+    steps = ((2, 2), (1, 2), (3, 2), (2, 1), (2, 3), (0, 2), (2, 0), (1, 1), (3, 3), (1, 3), (3, 1), (0, 1), (0, 3), (1, 0), (3, 0))
     along = (x, y, z, z)
     place = (4 * z + y, 4 * z + x, 4 * y + x, 4 * y + x)
 
@@ -115,6 +115,9 @@
                 if 0 < (dx > 0) + (dy > 0) + (dz > 0) < 3:
                     to = device(lax.rem(x + dx, 4), lax.rem(y + dy, 4), lax.rem(z + dz, 4))
                     pl.semaphore_signal(barrier, inc=1, device_id=to, device_id_type=MESH)
+
+    for load in loads:
+        load.start()
 
     def prepare(s):
         j = 2 * along[s] + e
@@ -180,7 +183,8 @@
                 part[s, :, order[t][u], k] = acc[:, u * 128:u * 128 + 128].reshape(16, 8, 128)
 
     def w2(s, d, first, count, to_buf, sem):
-        to = lax.rem(place[s] + d, 16)
+        da, db = steps[d - 1]
+        to = 4 * lax.rem(place[s] // 4 + da, 4) + lax.rem(place[s] + db, 4)
         return remote(part.at[s, to, first:first + count], to_buf.at[place[s]], w2s.at[sem], w2r.at[sem], plane(s, to))
 
     def w2_wait(buf, sem):
@@ -319,6 +323,8 @@
             ud, li = diag_factor(x_ref[lo:hi, lo:hi])
             inverses.append(li)
             if n == 2:
+                others(1)
+                others(3)
                 panel_rest(1)
                 for k in range(4):
                     x_ref[k * 128:k * 128 + 128, 640:768] = blk(1, kr, k).T
@@ -341,9 +347,6 @@
             if n == 1:
                 panel_half(1)
                 others(2)
-            if n == 2:
-                others(1)
-                others(3)
             if n == 3:
                 pass
         at = pl.multiple_of(kc * 128, 128)

time: 64 us -> 63.8 us (level)
  no operation moved by 1% of the time
where the time goes in v6:
time: 63.8 us; the launch traced here: 63.6 us
  Pallas kernels  61.1 us (96%)
  local copies, waits for them, and re-layouts  1.87 us (3%)
  between operations  0.66 us (1%)
    pallas_call x1, Pallas kernels, body(): pl.pallas_call(kernel, out_shape=jax.ShapeDtypeStruct((512, 256), jnp.flo...  61.1 us
    unnamed x1, local copies, waits for them, and re-layouts  1.87 us

profile of v6, /device:TPU:0, one launch (start us, length us, event | category | flops | bytes accessed | tf_op | source)
XLA Modules:
  0.0 63.6 jit_solution(9338390147922513634)
XLA Ops:
  0.7 61.1 %shard_map.64 = f32[512,256]{1,0:T(8,128)} custom-call(bf16[4,4,128,128]{3,2,1,0:T(8,128)(2,1)} %data_h.1, bf16[4,128]{1,0:T(4,128)(2,1)} %scale_h.1, s32[4,4]{1,0:T(4,128)} %ids_h.1, s32[4]{0:T(128)} %live_rows_h.1, s32[1]{0:T(128)S(6)} %copy.8.live_blocks_h, f32[32,128]{1,0:T(8,128)} %bitcast.1), custom_call_target="tpu_custom_call" | custom-call | tf_op jit(solution)/shard_map/pallas_call | solution.py:414
  61.8 1.9 %copy.9 = f32[512,256]{1,0:T(8,128)} copy(f32[512,256]{1,0:T(8,128)} %shard_map.64) | data formatting | bytes 1048576

commit v7 on v6

--- a/solution.py
+++ b/solution.py
@@ -203,7 +203,8 @@
 
     def to_panel(t):
         for d in range(8):
-            to = ((d // 4) * 2 + (d // 2) % 2, (d % 2) * 2 + 1 - e)
+            c = lax.rem(place[0] + d, 8)
+            to = ((c // 4) * 2 + lax.rem(c // 2, 2), lax.rem(c, 2) * 2 + 1 - e)
             remote(res.at[0, t], panel.at[e, t, xl, xh, place[0]], ps.at[t], pr.at[t], to).start()
 
     def panel_sent(t):

time: 63.8 us -> 63.5 us (level)
  no operation moved by 1% of the time
where the time goes in v7:
time: 63.5 us; the launch traced here: 63.3 us
  Pallas kernels  60.8 us (96%)
  local copies, waits for them, and re-layouts  1.87 us (3%)
  between operations  0.66 us (1%)
    pallas_call x1, Pallas kernels, body(): pl.pallas_call(kernel, out_shape=jax.ShapeDtypeStruct((512, 256), jnp.flo...  60.8 us
    unnamed x1, local copies, waits for them, and re-layouts  1.87 us

profile of v7, /device:TPU:0, one launch (start us, length us, event | category | flops | bytes accessed | tf_op | source)
XLA Modules:
  0.0 63.3 jit_solution(622886563153441432)
XLA Ops:
  0.7 60.8 %shard_map.64 = f32[512,256]{1,0:T(8,128)} custom-call(bf16[4,4,128,128]{3,2,1,0:T(8,128)(2,1)} %data_h.1, bf16[4,128]{1,0:T(4,128)(2,1)} %scale_h.1, s32[4,4]{1,0:T(4,128)} %ids_h.1, s32[4]{0:T(128)} %live_rows_h.1, s32[1]{0:T(128)S(6)} %copy.8.live_blocks_h, f32[32,128]{1,0:T(8,128)} %bitcast.1), custom_call_target="tpu_custom_call" | custom-call | tf_op jit(solution)/shard_map/pallas_call | solution.py:415
  61.5 1.9 %copy.9 = f32[512,256]{1,0:T(8,128)} copy(f32[512,256]{1,0:T(8,128)} %shard_map.64) | data formatting | bytes 1048576
